TPU v7x, 128 devices: a whole 4x4x4 slice. The times are simulated.
128 devices in a mesh: gx: 16 (over x, z_lo, core), gy: 8 (over y, z_hi).
Axes of the slice: x: 4, y: 4, z: 4 (z_hi: 2, z_lo: 2; z = z_hi * 2 + z_lo), core: 2. Of those that a mesh axis runs over, the one named last changes fastest.
Arguments:
- fine_input: float32 [64, 64, 128, 256], P(None, 'gx', 'gy'), may hold values from -34 to 34
- weights: float32 [27, 128, 64], replicated, may hold values from -0.15625 to 0.15625
- norm_gain: float32 [128], P(('gx', 'gy')), may hold values from 0.5 to 2
- norm_shift: float32 [128], P(('gx', 'gy')), may hold values from -3 to 3
- cotangent: float32 [128, 32, 64, 128], P(('gx', 'gy')), may hold values from -6 to 6
Outputs:
- activated: float32 [128, 32, 64, 128], P(('gx', 'gy'))
- grad_input: float32 [64, 64, 128, 256], P(None, 'gx', 'gy')
- grad_weights: float32 [27, 128, 64], replicated
- grad_gain: float32 [128], P(('gx', 'gy'))
- grad_shift: float32 [128], P(('gx', 'gy'))
All inputs are finite; a program needn't handle non-finite values.
Results may differ from a plain program's by a relative error of at most 0.00026.
Values sent between devices are 32-bit elements; how exact they have to be, the bound alone decides.
A program may use at most 128 MiB of HBM per device.

v0:
```python
import math

import jax
import jax.numpy as jnp
from jax import lax
from jax.sharding import PartitionSpec as P

epsilon = 1e-05
highest = lax.Precision.HIGHEST


def passed_along(block, axis, distance):
    devices = range(lax.axis_size(axis))
    route = [(i - distance, i) for i in devices if i - distance in devices]
    return lax.ppermute(block, axis, route)


def with_rims(volume, direction):
    slab_x = volume[:, -1:] if direction > 0 else volume[:, :1]
    arrived = passed_along(slab_x, "gx", direction)
    volume = jnp.concatenate([arrived, volume] if direction > 0 else [volume, arrived], axis=1)
    slab_y = volume[:, :, -1:] if direction > 0 else volume[:, :, :1]
    arrived = passed_along(slab_y, "gy", direction)
    return jnp.concatenate([arrived, volume] if direction > 0 else [volume, arrived], axis=2)


def parity_terms(parity):
    return [(1, 0)] if parity == 0 else [(0, 1), (2, 0)]


def next_along_z(volume):
    return jnp.pad(volume[..., 1:], ((0, 0), (0, 0), (0, 0), (0, 1)))


def local(fine_input, weights, norm_gain, norm_shift, cotangent):
    in_ch = fine_input.shape[0]
    out_ch = weights.shape[1]
    coarse_x, coarse_y, coarse_z = (
        fine_input.shape[1] // 2,
        fine_input.shape[2] // 2,
        fine_input.shape[3] // 2,
    )
    groups_x = lax.axis_size("gx")
    groups_y = lax.axis_size("gy")
    extended = jnp.pad(with_rims(fine_input, 1), ((0, 0), (0, 1), (0, 1), (0, 0)))
    split = extended.reshape(in_ch, coarse_x + 1, 2, coarse_y + 1, 2, coarse_z, 2)
    split = split.transpose(2, 4, 6, 0, 1, 3, 5)

    def fine_window(off_x, off_y, off_z):
        par_z = 0 if off_z == 1 else 1
        block = split[off_x % 2, off_y % 2, par_z]
        return block[:, off_x // 2 : off_x // 2 + coarse_x, off_y // 2 : off_y // 2 + coarse_y, :]

    conv_main = jnp.zeros((out_ch, coarse_x, coarse_y, coarse_z), jnp.float32)
    conv_prev = jnp.zeros((out_ch, coarse_x, coarse_y, coarse_z), jnp.float32)
    for off_x in range(3):
        for off_y in range(3):
            for off_z in range(3):
                term = jnp.einsum(
                    "oc,cxyz->oxyz",
                    weights[(off_x * 3 + off_y) * 3 + off_z],
                    fine_window(off_x, off_y, off_z),
                    precision=highest,
                )
                if off_z == 0:
                    conv_prev = conv_prev + term
                else:
                    conv_main = conv_main + term
    conv_local = conv_main + jnp.pad(conv_prev[..., :-1], ((0, 0), (0, 0), (0, 0), (1, 0)))
    moved = lax.all_to_all(conv_local, ("gx", "gy"), split_axis=0, concat_axis=1, tiled=True)
    kept = moved.shape[0]
    moved = moved.reshape(kept, groups_x, groups_y, coarse_x, coarse_y, coarse_z)
    conv = moved.transpose(0, 1, 3, 2, 4, 5).reshape(
        kept, groups_x * coarse_x, groups_y * coarse_y, coarse_z
    )
    average = jnp.mean(conv, axis=(1, 2, 3), keepdims=True)
    centred = conv - average
    spread = jnp.mean(centred * centred, axis=(1, 2, 3), keepdims=True)
    inv_std = 1.0 / jnp.sqrt(spread + epsilon)
    normed = centred * inv_std
    gain_col = norm_gain[:, None, None, None]
    pre = gain_col * normed + norm_shift[:, None, None, None]
    sig = jax.nn.sigmoid(pre)
    activated = pre * sig
    grad_pre = cotangent * sig * (1.0 + pre * (1.0 - sig))
    cells_count = conv.shape[1] * conv.shape[2] * conv.shape[3]
    rescale = 1.0 / math.sqrt(cells_count)
    grad_gain = jnp.sum(grad_pre * normed, axis=(1, 2, 3)) * rescale
    grad_shift = jnp.sum(grad_pre, axis=(1, 2, 3)) * rescale
    grad_norm = gain_col * grad_pre
    grad_conv = inv_std * (
        grad_norm
        - jnp.mean(grad_norm, axis=(1, 2, 3), keepdims=True)
        - normed * jnp.mean(grad_norm * normed, axis=(1, 2, 3), keepdims=True)
    )
    kept = grad_conv.shape[0]
    spread_out = grad_conv.reshape(kept, groups_x, coarse_x, groups_y, coarse_y, coarse_z)
    spread_out = spread_out.transpose(0, 1, 3, 2, 4, 5).reshape(
        kept, groups_x * groups_y * coarse_x, coarse_y, coarse_z
    )
    grad_local = lax.all_to_all(spread_out, ("gx", "gy"), split_axis=1, concat_axis=0, tiled=True)
    coarse_ext = with_rims(grad_local, -1)
    coarse_next = next_along_z(coarse_ext)
    parity_blocks = []
    for par_x in range(2):
        for par_y in range(2):
            for par_z in range(2):
                summed = jnp.zeros((in_ch, coarse_x, coarse_y, coarse_z), jnp.float32)
                for tap_x, move_x in parity_terms(par_x):
                    for tap_y, move_y in parity_terms(par_y):
                        for tap_z, move_z in parity_terms(par_z):
                            source = coarse_next if move_z == 1 else coarse_ext
                            window = source[
                                :, move_x : move_x + coarse_x, move_y : move_y + coarse_y, :
                            ]
                            summed = summed + jnp.einsum(
                                "oc,oxyz->cxyz",
                                weights[(tap_x * 3 + tap_y) * 3 + tap_z],
                                window,
                                precision=highest,
                            )
                parity_blocks.append(summed)
    stacked = jnp.stack(parity_blocks).reshape(2, 2, 2, in_ch, coarse_x, coarse_y, coarse_z)
    grad_input = stacked.transpose(3, 4, 0, 5, 1, 6, 2).reshape(
        in_ch, 2 * coarse_x, 2 * coarse_y, 2 * coarse_z
    )
    grad_next = next_along_z(grad_local)
    term_list = []
    for off_x in range(3):
        for off_y in range(3):
            for off_z in range(3):
                source = grad_next if off_z == 0 else grad_local
                term_list.append(
                    jnp.einsum(
                        "oxyz,cxyz->oc", source, fine_window(off_x, off_y, off_z), precision=highest
                    )
                )
    raw_w = lax.psum(jnp.stack(term_list), ("gx", "gy"))
    return (activated, grad_input, raw_w * rescale, grad_gain, grad_shift)


def solution(mesh):
    placed = (
        P(None, "gx", "gy", None),
        P(),
        P(("gx", "gy")),
        P(("gx", "gy")),
        P(("gx", "gy"), None, None, None),
    )
    return jax.shard_map(
        local,
        mesh=mesh,
        in_specs=placed,
        out_specs=(
            P(("gx", "gy"), None, None, None),
            P(None, "gx", "gy", None),
            P(),
            P(("gx", "gy")),
            P(("gx", "gy")),
        ),
        check_vma=False,
    )
```

profile of v0, /device:TPU:1, one launch (start us, length us, event | category | flops | bytes accessed | tf_op | source)
XLA Modules:
  0.0 476.8 jit_solution(18199161609801704225)
XLA Ops:
  9.3 4.9 %collective-permute-start = (f32[64,1,16,256]{3,0,2,1:T(8,128)S(1)}, f32[64,1,16,256]{3,0,2,1:T(8,128)S(1)}, u32[]{:S(2)}, u32[]{:S(2)}) collective-permute-start(f32[64,1,16,256]{3,0,2,1:T(8,128)S(1)} %copy.230), channel_id=1, source_target_pairs={{0,8},{8,16},{16,24},{24,32},{32,40},{40,48},{48,56},{56,64},{64,7... | collective-permute-start | bytes 3145736 | tf_op jit(solution)/shard_map/ppermute | solution.py:15
  14.2 13.5 %collective-permute-done = f32[64,1,16,256]{3,0,2,1:T(8,128)S(1)} collective-permute-done((f32[64,1,16,256]{3,0,2,1:T(8,128)S(1)}, f32[64,1,16,256]{3,0,2,1:T(8,128)S(1)}, u32[]{:S(2)}, u32[]{:S(2)}) %collective-permute-start) | collective-permute-done | bytes 1048608 | tf_op jit(solution)/shard_map/ppermute | solution.py:15
  27.8 2.7 constant_dynamic-update-slice_fusion
  30.5 3.5 collective-permute-start.1
  34.0 4.0 collective-permute-done.1
  38.0 3.1 pad_maximum_fusion
  41.1 8.9 %copy.175 = f32[64,5,17,256]{0,3,2,1:T(8,128)} copy(f32[64,5,17,256]{3,0,2,1:T(8,128)} %pad_maximum_fusion) | data formatting | bytes 11141120
  50.0 11.4 %pad.16.clone = f32[64,6,18,256]{0,3,2,1:T(8,128)} pad(f32[64,5,17,256]{0,3,2,1:T(8,128)} %copy.175, f32[]{:T(128)} %constant.20.clone.1), padding=0_0x0_1x0_1x0_0 | pad | bytes 12648452 | tf_op jit(solution)/shard_map/jit(_pad)/pad | solution.py:45
  61.3 19.4 %copy.85 = f32[64,3,2,9,2,128,2]{5,0,3,1,6,4,2:T(8,128)} copy(f32[64,3,2,9,2,128,2]{0,6,5,4,3,2,1:T(2,128)} %bitcast.647) | data formatting | bytes 14155776 | tf_op jit(solution)/shard_map/reshape | solution.py:46
  80.8 2.9 fusion.131
  83.7 3.0 fusion.142
  86.7 2.9 convolution_add_fusion.7
  89.5 2.9 convolution_add_fusion.6
  92.4 1.8 convolution_add_fusion.5
  94.2 1.8 convolution_add_fusion.4
  97.9 2.0 convolution_add_fusion.2
  99.8 1.8 convolution_add_fusion.1
  101.7 1.8 fusion.1
  103.5 1.8 convolution_add_fusion.23
  108.9 1.8 convolution_add_fusion.20
  110.7 2.2 convolution_add_fusion.19
  113.0 1.8 convolution_add_fusion.18
  123.9 2.0 convolution_add_fusion.12
  125.9 1.8 convolution_add_fusion.11
  133.1 1.8 fusion.3
  136.3 16.2 %all-to-all-start = ((f32[128,2,8,128]{3,2,1,0:T(8,128)}), f32[128,2,8,128]{3,2,1,0:T(8,128)S(1)}, u32[]{:S(2)}, u32[]{:S(2)}) async-start(f32[128,2,8,128]{3,2,1,0:T(8,128)} %copy.86), calls=%async_computation | async-start | bytes 2097152 | tf_op jit(solution)/shard_map/all_to_all | solution.py:70
  153.8 18.2 %all-to-all-done = f32[128,2,8,128]{3,2,1,0:T(8,128)S(1)} async-done(((f32[128,2,8,128]{3,2,1,0:T(8,128)}), f32[128,2,8,128]{3,2,1,0:T(8,128)S(1)}, u32[]{:S(2)}, u32[]{:S(2)}) %all-to-all-start) | async-done | bytes 1048608 | tf_op jit(solution)/shard_map/all_to_all | solution.py:70
  180.5 3.9 all-to-all-start.1
  184.9 5.8 %slice_bitcast_fusion.1 = (f32[64,3,9,128]{3,0,2,1:T(8,128)}, f32[64,3,9,128]{3,0,2,1:T(8,128)}, f32[64,3,9,128]{3,0,2,1:T(8,128)}, f32[64,3,9,128]{3,0,2,1:T(8,...) fusion(f32[2,2,2,64,3,9,128]{6,3,5,4,2,1,0:T(8,128)} %bitcast.623), kind=kLoop, calls=%fused_computation.147 | loop fusion | bytes 14155776 | tf_op jit(solution)/shard_map/squeeze | solution.py:51
  191.9 12.0 %all-to-all-done.1 = f32[1,256,8,128]{3,2,0,1:T(8,128)S(1)} async-done(((f32[1,256,8,128]{3,2,0,1:T(8,128)}), f32[1,256,8,128]{3,2,0,1:T(8,128)S(1)}, u32[]{:S(2)}, u32[]{:S(2)}) %all-to-all-start.1) | async-done | bytes 1048608 | tf_op jit(solution)/shard_map/all_to_all | solution.py:101
  205.5 2.6 fusion.31
  208.1 2.6 fusion.173
  210.6 2.6 fusion.168
  213.2 2.6 fusion.159
  215.8 2.6 fusion.154
  218.4 2.7 fusion.144
  223.3 2.0 fusion.57
  225.3 2.0 fusion.56
  229.1 2.2 fusion.54
  231.3 2.0 fusion.53
  235.2 2.0 fusion.51
  237.2 2.0 fusion.50
  241.0 2.0 fusion.48
  243.1 2.0 fusion.47
  246.9 2.0 fusion.45
  248.9 2.0 fusion.44
  252.7 2.4 fusion.42
  255.2 2.0 fusion.41
  259.0 2.0 fusion.39
  261.0 2.0 fusion.38
  264.9 2.0 fusion.36
  266.9 2.0 fusion.35
  270.7 2.0 fusion.33
  272.7 2.0 fusion.32
  274.8 2.0 copy.231
  276.8 2.2 collective-permute-start.2
  279.0 2.6 fusion.133
  281.6 2.5 fusion.114
  284.1 134.2 %all-reduce.6.cloned.1.call-done = f32[27,128,64]{1,2,0:T(8,128)} async-done(((f32[27,128,64]{1,2,0:T(8,128)}), f32[27,128,64]{1,2,0:T(8,128)}) %all-reduce.6.cloned.1.call-update) | async-done | bytes 884752 | tf_op jit(solution)/shard_map/psum | solution.py:138
  418.3 2.2 broadcast_multiply_fusion
  425.3 7.7 %collective-permute-done.3 = f32[128,3,1,128]{3,0,2,1:T(8,128)S(1)} collective-permute-done((f32[128,3,1,128]{3,0,2,1:T(8,128)S(1)}, f32[128,3,1,128]{3,0,2,1:T(8,128)S(1)}, u32[]{:S(2)}, u32[]{:S(2)}) %collective-permute-start.3) | collective-permute-done | bytes 196640 | tf_op jit(solution)/shard_map/ppermute | solution.py:15
  446.0 2.0 copy-done.6
  448.0 12.2 %copy.100 = f32[2,2,2,64,2,8,128]{3,2,6,1,5,0,4:T(2,128)} copy(f32[2,2,2,64,2,8,128]{6,3,5,4,2,1,0:T(8,128)} %bitcast.651) | data formatting | bytes 8388608 | tf_op jit(solution)/shard_map/reshape | solution.py:123
  460.2 7.3 %copy.120 = f32[64,4,16,256]{3,2,1,0:T(8,128)} copy(f32[64,4,16,256]{0,3,2,1:T(8,128)} %bitcast.648) | data formatting | bytes 8388608
  (103 shorter events, 65.3 us)
Async XLA Ops:
  7.2 20.6 %copy-start.4 = (f32[64,4,16,256]{3,2,1,0:T(8,128)S(1)}, f32[64,4,16,256]{3,2,1,0:T(8,128)}, u32[]{:S(2)}) copy-start(f32[64,4,16,256]{3,2,1,0:T(8,128)} %param.5) | copy-start | bytes 12582916
  9.3 18.4 %collective-permute-start = (f32[64,1,16,256]{3,0,2,1:T(8,128)S(1)}, f32[64,1,16,256]{3,0,2,1:T(8,128)S(1)}, u32[]{:S(2)}, u32[]{:S(2)}) collective-permute-start(f32[64,1,16,256]{3,0,2,1:T(8,128)S(1)} %copy.230), channel_id=1, source_target_pairs={{0,8},{8,16},{16,24},{24,32},{32,40},{40,48},{48,56},{56,64},{64,7... | collective-permute-start | bytes 3145736 | tf_op jit(solution)/shard_map/ppermute | solution.py:15
  30.5 7.5 %collective-permute-start.1 = (f32[64,5,1,256]{3,0,2,1:T(8,128)S(1)}, f32[64,5,1,256]{3,0,2,1:T(8,128)S(1)}, u32[]{:S(2)}, u32[]{:S(2)}) collective-permute-start(f32[64,5,1,256]{3,0,2,1:T(8,128)S(1)} %slice.390), channel_id=1, source_target_pairs={{0,1},{1,2},{2,3},{3,4},{4,5},{5,6},{6,7},{8,9},{9,10},{10,11},{11... | collective-permute-start | bytes 983048 | tf_op jit(solution)/shard_map/ppermute | solution.py:15
  61.3 19.5 %copy-start.10 = (f32[27,128,64]{1,2,0:T(8,128)S(1)}, f32[27,128,64]{1,2,0:T(8,128)}, u32[]{:S(2)}) copy-start(f32[27,128,64]{1,2,0:T(8,128)} %param.6) | copy-start | bytes 2654212
  83.6 8.8 %copy-start = (f32[64,3,2,9,2,128,2]{5,0,3,1,6,4,2:T(8,128)S(1)}, f32[64,3,2,9,2,128,2]{5,0,3,1,6,4,2:T(8,128)}, u32[]{:S(2)}) copy-start(f32[64,3,2,9,2,128,2]{5,0,3,1,6,4,2:T(8,128)} %copy.85) | copy-start | bytes 21233668
  136.3 39.0 %copy-start.20 = (f32[1,32,64,128]{3,2,1,0:T(8,128)S(1)}, f32[1,32,64,128]{3,2,1,0:T(8,128)}, u32[]{:S(2)}) copy-start(f32[1,32,64,128]{3,2,1,0:T(8,128)} %param.9) | copy-start | bytes 3145732
  136.3 35.7 %all-to-all-start = ((f32[128,2,8,128]{3,2,1,0:T(8,128)}), f32[128,2,8,128]{3,2,1,0:T(8,128)S(1)}, u32[]{:S(2)}, u32[]{:S(2)}) async-start(f32[128,2,8,128]{3,2,1,0:T(8,128)} %copy.86), calls=%async_computation | async-start | bytes 2097152 | tf_op jit(solution)/shard_map/all_to_all | solution.py:70
  180.5 23.5 %all-to-all-start.1 = ((f32[1,256,8,128]{3,2,0,1:T(8,128)}), f32[1,256,8,128]{3,2,0,1:T(8,128)S(1)}, u32[]{:S(2)}, u32[]{:S(2)}) async-start(f32[1,256,8,128]{3,2,0,1:T(8,128)} %bitcast.102), calls=%async_computation.1 | async-start | bytes 2097152 | tf_op jit(solution)/shard_map/all_to_all | solution.py:101
  184.5 233.9 %all-reduce.6.cloned.1.call-start = ((), (), s32[]{:S(2)}) async-start(), calls=%async_computation.2 | async-start | bytes 1769472 | tf_op jit(solution)/shard_map/psum | solution.py:138
  213.2 10.0 %copy-start.1 = (f32[64,3,9,128]{3,0,2,1:T(8,128)S(1)}, f32[64,3,9,128]{3,0,2,1:T(8,128)}, u32[]{:S(2)}) copy-start(f32[64,3,9,128]{3,0,2,1:T(8,128)} %get-tuple-element.32) | copy-start | bytes 2654212
  218.4 8.9 %copy-start.2 = (f32[64,3,9,128]{3,0,2,1:T(8,128)S(1)}, f32[64,3,9,128]{3,0,2,1:T(8,128)}, u32[]{:S(2)}) copy-start(f32[64,3,9,128]{3,0,2,1:T(8,128)} %get-tuple-element.29) | copy-start | bytes 2654212
  221.1 8.0 %copy-start.7 = (f32[64,3,9,128]{3,0,2,1:T(8,128)S(1)}, f32[64,3,9,128]{3,0,2,1:T(8,128)}, u32[]{:S(2)}) copy-start(f32[64,3,9,128]{3,0,2,1:T(8,128)} %get-tuple-element.30) | copy-start | bytes 2654212
  229.1 10.1 %copy-start.3 = (f32[64,3,9,128]{3,0,2,1:T(8,128)S(1)}, f32[64,3,9,128]{3,0,2,1:T(8,128)}, u32[]{:S(2)}) copy-start(f32[64,3,9,128]{3,0,2,1:T(8,128)} %get-tuple-element.27) | copy-start | bytes 2654212
  231.3 9.7 %copy-start.8 = (f32[64,3,9,128]{3,0,2,1:T(8,128)S(1)}, f32[64,3,9,128]{3,0,2,1:T(8,128)}, u32[]{:S(2)}) copy-start(f32[64,3,9,128]{3,0,2,1:T(8,128)} %get-tuple-element.28) | copy-start | bytes 2654212
  235.2 9.9 %copy-start.9 = (f32[64,3,9,128]{3,0,2,1:T(8,128)S(1)}, f32[64,3,9,128]{3,0,2,1:T(8,128)}, u32[]{:S(2)}) copy-start(f32[64,3,9,128]{3,0,2,1:T(8,128)} %get-tuple-element.26) | copy-start | bytes 2654212
  237.2 9.7 %copy-start.12 = (f32[64,3,9,128]{3,0,2,1:T(8,128)S(1)}, f32[64,3,9,128]{3,0,2,1:T(8,128)}, u32[]{:S(2)}) copy-start(f32[64,3,9,128]{3,0,2,1:T(8,128)} %get-tuple-element.25) | copy-start | bytes 2654212
  274.8 146.8 %copy-start.11 = (f32[27,128,64]{1,2,0:T(8,128)S(1)}, f32[27,128,64]{1,2,0:T(8,128)}, u32[]{:S(2)}) copy-start(f32[27,128,64]{1,2,0:T(8,128)} %param.6) | copy-start | bytes 2654212
  276.8 143.7 %collective-permute-start.2 = (f32[128,1,8,128]{3,0,2,1:T(8,128)}, f32[128,1,8,128]{3,0,2,1:T(8,128)}, u32[]{:S(2)}, u32[]{:S(2)}) collective-permute-start(f32[128,1,8,128]{3,0,2,1:T(8,128)} %copy.231), channel_id=1, source_target_pairs={{8,0},{16,8},{24,16},{32,24},{40,32},{48,40},{56,48},{64,56},{72,6... | collective-permute-start | bytes 1572872 | tf_op jit(solution)/shard_map/ppermute | solution.py:15
  423.1 9.9 %collective-permute-start.3 = (f32[128,3,1,128]{3,0,2,1:T(8,128)S(1)}, f32[128,3,1,128]{3,0,2,1:T(8,128)S(1)}, u32[]{:S(2)}, u32[]{:S(2)}) collective-permute-start(f32[128,3,1,128]{3,0,2,1:T(8,128)S(1)} %slice.401), channel_id=1, source_target_pairs={{1,0},{2,1},{3,2},{4,3},{5,4},{6,5},{7,6},{9,8},{10,9},{11,10},{12... | collective-permute-start | bytes 589832 | tf_op jit(solution)/shard_map/ppermute | solution.py:15
  434.3 3.1 copy-start.5
  434.3 3.1 copy-start.16
  436.6 2.3 copy-start.15
  437.3 2.3 copy-start.18
  438.1 2.3 copy-start.14
  438.9 2.3 copy-start.17
  442.0 2.2 copy-start.19
  442.7 2.3 copy-start.13
  446.0 2.0 copy-start.6
Sparse Core Ops, SparseCore 0:
  274.9 143.3 all-reduce.5
where the time goes:
time: 483 us; the launch traced here: 477 us
  waiting for transfers between devices  190 us (39%)
  matrix products  142 us (29%)
  local copies, waits for them, and re-layouts  79.5 us (16%)
  starting transfers between devices  32.6 us (7%)
  between operations  22.4 us (5%)
  other arithmetic  10.4 us (2%)
    psum x1, waiting for transfers between devices, local(): raw_w = lax.psum(jnp.stack(term_list), ('gx', 'gy'))  134 us
    dot_general x27, matrix products, local(): jnp.einsum('oc,cxyz->oxyz', weights[(off_x * 3 + off_y) * 3 + off_z], fin...  53.9 us
    dot_general x27, matrix products, local(): jnp.einsum('oxyz,cxyz->oc', source, fine_window(off_x, off_y, off_z), pre...  53.3 us
    dot_general x27, matrix products, local(): jnp.einsum('oc,oxyz->cxyz', weights[(tap_x * 3 + tap_y) * 3 + tap_z], win...  35 us
    ppermute x4, waiting for transfers between devices, passed_along(): return lax.ppermute(block, axis, route)  25.2 us
    unnamed x49, local copies, waits for them, and re-layouts  21.7 us
    reshape x1, local copies, waits for them, and re-layouts, local(): extended.reshape(in_ch, coarse_x + 1, 2, coarse_y + 1, 2, coarse_z, 2)  19.4 us
    all_to_all x1, waiting for transfers between devices, local(): lax.all_to_all(conv_local, ('gx', 'gy'), split_axis=0, concat_axis=1, til...  18.2 us
  transfers between devices with their start and end apart: 7, of which 6 were waited for; matrix products, arithmetic and copies ran while one was open for 3% of the time, Pallas kernels for 0%

commit v1 on v0

v1 whole, which is shorter than its diff:
```python
import functools
import math

import jax
import jax.numpy as jnp
from jax import lax
from jax.experimental import pallas as pl
from jax.experimental.pallas import tpu as pltpu
from jax.sharding import PartitionSpec as P

MESH = pl.DeviceIdType.MESH
F32 = jnp.float32
BF16 = jnp.bfloat16
GX, GY, N_DEV = 16, 8, 128
CI, CO = 64, 128
CELLS = 32 * 64 * 128
OWN_CELLS = CELLS // N_DEV
RESCALE = 1.0 / math.sqrt(CELLS)
EPSILON = 1e-5
SLICE_OWNERS = 27 * CI // 16


def dot(a, b):
    return jnp.dot(a, b, preferred_element_type=F32)


def dot_nt(a, b):
    return lax.dot_general(a, b, (((1,), (1,)), ((), ())), preferred_element_type=F32)


def high_low(value):
    high = value.astype(BF16)
    return high, (value - high.astype(F32)).astype(BF16)


def rows_to_columns(rows):
    return jnp.concatenate([rows, jnp.zeros((120, 128), F32)], axis=0).T


def kernel(
    fine, wts, gain, shift, cot, act_out, gin_out, gw_out, gg_out, gs_out,
    fine_v, w_v, cot_v, x_hi, x_lo, even_t, odd_t, wf_e, wf_o, wb, conv, conv_t, rim_x, rim_y, rim_c,
    g_f, g_w, g_i, o_acc, out_v, act_v, stat, stat_x, stat_y, wg, wg_in, wg_all,
    local_sem, out_sem, cot_send, cot_recv, rim_send, rim_recv, stat_send, stat_recv,
    act_send, act_recv, g_send, g_recv, wr_send, wr_recv, wa_send, wa_recv,
):
    gx, gy = lax.axis_index("gx"), lax.axis_index("gy")
    me = gx * GY + gy

    def at(lin):
        return (lin // GY, lax.rem(lin, GY))

    def remote(src, dst, send, recv, device):
        return pltpu.make_async_remote_copy(
            src_ref=src, dst_ref=dst, send_sem=send, recv_sem=recv,
            device_id=device, device_id_type=MESH,
        )

    fine_in = [
        pltpu.make_async_copy(fine.at[:, x], fine_v.at[x], local_sem.at[x]) for x in (3, 2, 1, 0)
    ]
    for copy in fine_in:
        copy.start()
    w_in = pltpu.make_async_copy(wts, w_v, local_sem.at[4])
    w_in.start()
    my_cells = (pl.ds(2 * gx, 2), pl.ds(pl.multiple_of(8 * gy, 8), 8), slice(None))
    cot_own = pltpu.make_async_copy(cot.at[(0,) + my_cells], cot_v.at[me], local_sem.at[5])
    cot_own.start()

    barrier = pltpu.get_barrier_semaphore()

    def greet(k, carry):
        pl.semaphore_signal(
            barrier, inc=1, device_id=at(lax.rem(me + k, N_DEV)), device_id_type=MESH
        )
        return carry

    lax.fori_loop(1, N_DEV, greet, 0)

    row = lax.broadcasted_iota(jnp.int32, (256, 256), 0)
    col = lax.broadcasted_iota(jnp.int32, (256, 256), 1)
    split = jnp.where(
        row == jnp.where(col < 128, 2 * col, 2 * (col - 128) + 1), 1.0, 0.0
    ).astype(BF16)
    merge = jnp.where(
        col == jnp.where(row < 128, 2 * row, 2 * (row - 128) + 1), 1.0, 0.0
    ).astype(BF16)
    lane = lax.broadcasted_iota(jnp.int32, (64, 128), 1)

    w_in.wait()
    for b in range(3):
        flat = jnp.concatenate([w_v[(a * 3 + b) * 3 + c] for a in range(3) for c in range(3)], axis=1)
        high, low = high_low(flat)
        if b == 1:
            wf_e[0:128], wf_e[128:256] = high, low
        else:
            at_row = 0 if b == 2 else 128
            wf_o[at_row : at_row + 128] = high
            wf_o[256 + at_row : 384 + at_row] = low

    pl.semaphore_wait(barrier, N_DEV - 1)

    def send_cot(k, carry):
        to = lax.rem(me + k, N_DEV)
        tx, ty = at(to)
        src = cot.at[0, pl.ds(2 * tx, 2), pl.ds(pl.multiple_of(8 * ty, 8), 8), :]
        remote(src, cot_v.at[me], cot_send, cot_recv, (tx, ty)).start()
        return carry

    lax.fori_loop(1, N_DEV, send_cot, 0)

    def split_slab(x):
        high, low = high_low(fine_v[x].reshape(CI * 16, 256))
        for part, dst in ((high, x_hi), (low, x_lo)):
            both = dot(part, split)
            even_t[...] = both[:, :128]
            odd_t[...] = both[:, 128:]

            def one_row(y, carry, dst=dst):
                half, cell = lax.rem(y, 2), y // 2
                even = even_t[pl.ds(y, CI, stride=16), :]
                odd = odd_t[pl.ds(y, CI, stride=16), :]
                before = jnp.where(lane == 0, 0.0, pltpu.roll(odd, 1, 1))
                lanes = pl.ds(pl.multiple_of(cell * 128, 128), 128)
                dst[half, x * 192 : x * 192 + 64, lanes] = before.astype(BF16)
                dst[half, x * 192 + 64 : x * 192 + 128, lanes] = even.astype(BF16)
                dst[half, x * 192 + 128 : x * 192 + 192, lanes] = odd.astype(BF16)
                return carry

            lax.fori_loop(0, 16, one_row, 0)

    def forward(mx):
        x0, x1 = ((0, 2), (1, 4), (3, 4))[mx]
        a0 = (1, 0, 0)[mx]
        rows = slice(x0 * 192, x1 * 192)
        depth = (x1 - x0) * 192
        cols = slice(a0 * 192, a0 * 192 + depth)
        conv[mx, :, 0:128] = jnp.zeros((CO, 128), F32)

        def chunk(n, carry):
            here = pl.ds(pl.multiple_of(n * 256, 256), 256)
            e_hi, e_lo = x_hi[0, rows, here], x_lo[0, rows, here]
            o_hi, o_lo = x_hi[1, rows, here], x_lo[1, rows, here]
            e = dot(wf_e[:, cols], e_hi)
            e = e[:128] + e[128:] + dot(wf_e[0:128, cols], e_lo)
            o = dot(wf_o[:, cols], o_hi)
            o = o[:256] + o[256:] + dot(wf_o[0:256, cols], o_lo)
            e = e + o[:128]
            first = pl.ds(pl.multiple_of(n * 256, 256), 128)
            second = pl.ds(pl.multiple_of(n * 256 + 128, 128), 128)
            conv[mx, :, first] += e[:, :128]
            conv[mx, :, second] = e[:, 128:] + o[128:, :128]
            conv[mx, :, pl.ds(pl.multiple_of(n * 256 + 256, 256), 128)] = o[128:, 128:]
            return carry

        lax.fori_loop(0, 4, chunk, 0)

    right = (lax.rem(gx + 1, GX), gy)
    up = (gx, lax.rem(gy + 1, GY))
    right_up = (lax.rem(gx + 1, GX), lax.rem(gy + 1, GY))
    left = (lax.rem(gx + GX - 1, GX), gy)
    down = (gx, lax.rem(gy + GY - 1, GY))
    left_down = (lax.rem(gx + GX - 1, GX), lax.rem(gy + GY - 1, GY))

    fine_in[0].wait()
    split_slab(3)
    forward(2)
    rims = [
        remote(conv.at[2, :, pl.ds(0, 1024)], rim_x, rim_send.at[0], rim_recv.at[0], right),
        remote(conv.at[2, :, pl.ds(1024, 128)], rim_c, rim_send.at[1], rim_recv.at[1], right_up),
    ]
    rims[0].start()
    rims[1].start()
    for i, x in ((1, 2), (2, 1), (3, 0)):
        fine_in[i].wait()
        split_slab(x)
    forward(1)
    forward(0)
    rims.append(
        remote(conv.at[pl.ds(0, 2), :, pl.ds(1024, 128)], rim_y, rim_send.at[2], rim_recv.at[2], up)
    )
    rims[2].start()

    for tap in range(9):
        turned = [w_v[tap * 3 + c].T for c in range(3)]
        for half, (now, later) in enumerate(((turned[1], None), (turned[2], turned[0]))):
            rows = slice(tap * 128 + half * 64, tap * 128 + half * 64 + 64)
            for k, block in enumerate((now, later)):
                if block is None:
                    high = low = jnp.zeros((64, 128), BF16)
                else:
                    high, low = high_low(block)
                wb[rows, k * 128 : k * 128 + 128] = high
                wb[rows, 256 + k * 128 : 384 + k * 128] = high
                wb[rows, 512 + k * 128 : 640 + k * 128] = low

    for copy in rims:
        copy.wait()
    has_left = jnp.where(gx > 0, 1.0, 0.0)
    has_down = jnp.where(gy > 0, 1.0, 0.0)
    conv[0, :, 0:1024] += rim_x[...] * has_left
    conv[0, :, 0:128] += rim_c[...] * (has_left * has_down)
    for mx in range(2):
        conv[mx, :, 0:128] += rim_y[mx] * has_down

    own = [conv[mx, :, 128 * my : 128 * my + 128] for mx in range(2) for my in range(8)]
    average = jnp.sum(functools.reduce(jnp.add, own), axis=1, keepdims=True) * (1.0 / OWN_CELLS)
    spread = jnp.sum(
        functools.reduce(jnp.add, [(v - average) * (v - average) for v in own]), axis=1, keepdims=True
    )
    wide = lax.broadcasted_iota(jnp.int32, (128, 128), 1)
    stat[0] = jnp.where(wide == 0, average, jnp.where(wide == 1, spread, 0.0)).T[0:8]
    one_row = lax.broadcasted_iota(jnp.int32, (1, 128), 1)
    mine = one_row == me
    stat[0, 2:3] = jnp.where(mine, gain[0], 0.0)
    stat[0, 3:4] = jnp.where(mine, shift[0], 0.0)

    def exchange(k, combine):
        def to_x(d, carry):
            t = lax.rem(gx + d, GX)
            remote(stat.at[2 * k], stat_x.at[k, gx], stat_send.at[2 * k], stat_recv.at[2 * k], (t, gy)).start()
            return carry

        lax.fori_loop(1, GX, to_x, 0)
        stat_x[k, pl.ds(gx, 1)] = stat[pl.ds(2 * k, 1)]
        everyone = stat_x.at[k, pl.ds(0, GX - 1)]
        remote(everyone, everyone, stat_send.at[2 * k], stat_recv.at[2 * k], right).wait()
        stat[2 * k + 1] = combine(stat_x[k], GX, OWN_CELLS)

        def to_y(d, carry):
            t = lax.rem(gy + d, GY)
            remote(stat.at[2 * k + 1], stat_y.at[k, gy], stat_send.at[2 * k + 1], stat_recv.at[2 * k + 1], (gx, t)).start()
            return carry

        lax.fori_loop(1, GY, to_y, 0)
        stat_y[k, pl.ds(gy, 1)] = stat[pl.ds(2 * k + 1, 1)]
        everyone = stat_y.at[k, pl.ds(0, GY - 1)]
        remote(everyone, everyone, stat_send.at[2 * k + 1], stat_recv.at[2 * k + 1], up).wait()
        return combine(stat_y[k], GY, OWN_CELLS * GX)

    def combine_moments(parts, count, cells):
        total = jnp.sum(parts, axis=0)
        mean = total[0:1] * (1.0 / count)
        away = functools.reduce(
            jnp.add, [(parts[i, 0:1] - mean) * (parts[i, 0:1] - mean) for i in range(count)]
        )
        return jnp.concatenate([mean, total[1:2] + cells * away, total[2:4], jnp.zeros((4, 128), F32)], axis=0)

    def combine_sums(parts, count, cells):
        return jnp.sum(parts, axis=0)

    moments = exchange(0, combine_moments)
    inv_row = 1.0 / jnp.sqrt(moments[1:2] * (1.0 / CELLS) + EPSILON)
    rows = jnp.concatenate([moments[0:1], inv_row, moments[2:4], jnp.zeros((4, 128), F32)], axis=0)
    columns = rows_to_columns(rows)
    average, inv_std = columns[:, 0:1], columns[:, 1:2]
    gain_col, shift_col = columns[:, 2:3], columns[:, 3:4]

    cot_own.wait()
    everyone = cot_v.at[pl.ds(0, N_DEV - 1)]
    remote(everyone, everyone, cot_send, cot_recv, right).wait()
    cot_rows = cot_v.reshape(CO * 16, 128)
    conv_rows = conv_t.reshape(CO * 16, 128)

    sums = jnp.zeros((128, 128), F32), jnp.zeros((128, 128), F32)
    for mx in range(2):

        def one_cell(my, carry, mx=mx):
            s0, s1 = carry
            lanes = pl.ds(pl.multiple_of(my * 128, 128), 128)
            value = conv[mx, :, lanes]
            normed = (value - average) * inv_std
            pre = gain_col * normed + shift_col
            sig = 1.0 / (1.0 + jnp.exp(-pre))
            conv_rows[pl.ds(mx * 8 + my, 128, stride=16), :] = pre * sig
            grad = cot_rows[pl.ds(mx * 8 + my, 128, stride=16), :] * sig * (1.0 + pre * (1.0 - sig))
            g_f[mx, :, lanes] = grad
            return s0 + grad, s1 + grad * normed

        sums = lax.fori_loop(0, 8, one_cell, sums)
    stat[2] = jnp.concatenate(
        [jnp.sum(s.T, axis=0, keepdims=True) for s in sums] + [jnp.zeros((6, 128), F32)], axis=0
    )
    totals = exchange(1, combine_sums)
    gs_out[...] = jnp.sum(jnp.where(mine, totals[0:1], 0.0), axis=1, keepdims=True) * RESCALE
    gg_out[...] = jnp.sum(jnp.where(mine, totals[1:2], 0.0), axis=1, keepdims=True) * RESCALE
    columns2 = rows_to_columns(totals)
    mean_g = gain_col * columns2[:, 0:1] * (1.0 / CELLS)
    mean_gn = gain_col * columns2[:, 1:2] * (1.0 / CELLS)

    def place(mx, lanes, value):
        high, low = high_low(value)
        g_w[mx, 0:128, lanes] = high
        g_w[mx, 128:256, lanes] = low
        g_i[mx, 0:128, lanes] = high
        g_i[mx, 256:384, lanes] = low
        g_i[mx, 512:640, lanes] = high
        moved = jnp.where(wide == 127, 0.0, pltpu.roll(value, 127, 1))
        high, low = high_low(moved)
        g_i[mx, 128:256, lanes] = high
        g_i[mx, 384:512, lanes] = low
        g_i[mx, 640:768, lanes] = high

    for mx in range(2):

        def finish(my, carry, mx=mx):
            lanes = pl.ds(pl.multiple_of(my * 128, 128), 128)
            normed = (conv[mx, :, lanes] - average) * inv_std
            value = inv_std * (gain_col * g_f[mx, :, lanes] - mean_g - normed * mean_gn)
            g_f[mx, :, lanes] = value
            place(mx, lanes, value)
            return carry

        lax.fori_loop(0, 8, finish, 0)

    g_rims = [
        remote(g_f.at[0, :, pl.ds(0, 1024)], g_f.at[2, :, pl.ds(0, 1024)], g_send.at[0], g_recv.at[0], left),
        remote(g_f.at[pl.ds(0, 2), :, pl.ds(0, 128)], g_f.at[pl.ds(0, 2), :, pl.ds(1024, 128)], g_send.at[1], g_recv.at[1], down),
        remote(g_f.at[0, :, pl.ds(0, 128)], g_f.at[2, :, pl.ds(1024, 128)], g_send.at[2], g_recv.at[2], left_down),
    ]
    for copy in g_rims:
        copy.start()

    def send_act(k, carry):
        to = lax.rem(me + k, N_DEV)
        remote(conv_t.at[to], act_v.at[my_cells], act_send, act_recv, at(to)).start()
        return carry

    lax.fori_loop(1, N_DEV, send_act, 0)
    act_own = pltpu.make_async_copy(conv_t.at[me], act_v.at[my_cells], local_sem.at[6])
    act_own.start()

    for copy in g_rims:
        copy.wait()
    has_right = jnp.where(gx < GX - 1, 1.0, 0.0)
    has_up = jnp.where(gy < GY - 1, 1.0, 0.0)

    def finish_x(my, carry):
        lanes = pl.ds(pl.multiple_of(my * 128, 128), 128)
        place(2, lanes, g_f[2, :, lanes] * has_right)
        return carry

    lax.fori_loop(0, 8, finish_x, 0)
    for mx, there in ((0, has_up), (1, has_up), (2, has_up * has_right)):
        place(mx, slice(1024, 1152), g_f[mx, :, 1024:1152] * there)

    for a in range(3):
        for b in range(3):
            half = 0 if b == 1 else 1
            first_lane = 128 if b == 0 else 0
            total = jnp.zeros((192, 128), F32)
            for x, mx in ((1, 1), (3, 2)) if a == 0 else ((a - 1, 0), (a + 1, 1)):
                rows = slice(x * 192, x * 192 + 192)
                g_here = g_w[mx, :, first_lane : first_lane + 1024]
                both = dot_nt(x_hi[half, rows, :], g_here)
                total += both[:, :128] + both[:, 128:] + dot_nt(x_lo[half, rows, :], g_here[:128])
            tap = (a * 3 + b) * 3
            wg[tap * 64 : tap * 64 + 192] = total

    def send_part(k, carry):
        to = lax.rem(me + k, N_DEV)

        @pl.when(to < SLICE_OWNERS)
        def _():
            src = wg.at[pl.ds(pl.multiple_of(to * 16, 16), 16)]
            remote(src, wg_in.at[me], wr_send, wr_recv, at(to)).start()

        return carry

    lax.fori_loop(1, N_DEV, send_part, 0)

    def add_to(x, half, lanes, value, fresh):
        if fresh:
            o_acc[x, half, :, lanes] = value
        else:
            o_acc[x, half, :, lanes] += value

    for mx in range(3):
        taps = [a for a in range(3) if 0 <= 2 * mx - 1 + a <= 3]
        top, bottom = taps[0] * 384, taps[-1] * 384 + 384

        for a in taps:
            rows = slice(a * 384, a * 384 + 128)
            value = dot(wb[rows, :], g_i[mx, :, 1024:1152])
            add_to(2 * mx - 1 + a, 1, slice(896, 1024), value, a > 0)

        def chunk(n, carry, mx=mx, taps=taps, top=top, bottom=bottom):
            n = 3 - n
            here = pl.ds(pl.multiple_of(n * 256, 256), 256)
            terms = dot(wb[top:bottom, :], g_i[mx, :, here])
            first = pl.ds(pl.multiple_of(n * 256, 256), 128)
            for a in taps:
                x = 2 * mx - 1 + a
                block = terms[a * 384 - top : a * 384 - top + 384]
                add_to(x, 0, here, block[128:256], a > 0)
                value = block[256:384]
                lanes2 = pl.ds(pl.multiple_of(n * 256 + 128, 128), 128)
                o_acc[x, 1, :, lanes2] += value[:, 128:]
                add_to(x, 1, first, value[:, :128] + block[0:128, 128:], a > 0)

                @pl.when(n > 0)
                def _(x=x, block=block, a=a):
                    add_to(x, 1, pl.ds(pl.multiple_of(n * 256 - 128, 128), 128), block[0:128, :128], a > 0)

            return carry

        lax.fori_loop(0, 4, chunk, 0)

    copies = []
    for x in range(4):
        slot = x % 2
        if x >= 2:
            for copy in copies[2 * (x - 2) : 2 * (x - 2) + 2]:
                copy.wait()
        for half in range(2):
            blocks = [
                jnp.concatenate(
                    [o_acc[x, half, 0:64, 128 * my : 128 * my + 128], o_acc[x, half, 64:128, 128 * my : 128 * my + 128]],
                    axis=1,
                )
                for my in range(8)
            ]
            high, low = high_low(jnp.concatenate(blocks, axis=0))
            merged = dot(high, merge) + dot(low, merge)
            for my in range(8):
                for z in range(2):
                    out_v[slot, z, pl.ds(2 * my + half, 64, stride=16), :] = merged[
                        64 * my : 64 * my + 64, 128 * z : 128 * z + 128
                    ]
        for z in range(2):
            copy = pltpu.make_async_copy(
                out_v.at[slot, z].reshape(CI, 16, 128),
                gin_out.at[:, x, :, pl.ds(128 * z, 128)],
                out_sem.at[slot, z],
            )
            copy.start()
            copies.append(copy)

    @pl.when(me < SLICE_OWNERS)
    def _():
        wg_in[pl.ds(me, 1)] = wg[pl.ds(pl.multiple_of(me * 16, 16), 16)][None]
        everyone = wg_in.at[pl.ds(0, N_DEV - 1)]
        remote(everyone, everyone, wr_send, wr_recv, right).wait_recv()
        wg_all[pl.ds(pl.multiple_of(me * 16, 16), 16)] = jnp.sum(wg_in[...], axis=0) * RESCALE

        def send_slice(k, carry):
            to = lax.rem(me + k, N_DEV)
            src = wg_all.at[pl.ds(pl.multiple_of(me * 16, 16), 16)]
            remote(src, src, wa_send, wa_recv, at(to)).start()
            return carry

        lax.fori_loop(1, N_DEV, send_slice, 0)
        some = wg.at[pl.ds(0, 16 * (SLICE_OWNERS - 1))]
        remote(some, some, wr_send, wr_recv, right).wait_send()
        everyone = wg_in.at[pl.ds(0, N_DEV - 1)]
        remote(everyone, everyone, wa_send, wa_recv, right).wait_send()
        some = wg_all.at[pl.ds(0, 16 * (SLICE_OWNERS - 1))]
        remote(some, some, wa_send, wa_recv, right).wait_recv()

    @pl.when(me >= SLICE_OWNERS)
    def _():
        remote(wg, wg, wr_send, wr_recv, right).wait_send()
        remote(wg_all, wg_all, wa_send, wa_recv, right).wait_recv()

    for tap in range(27):
        gw_out[tap] = wg_all[tap * 64 : tap * 64 + 64].T

    act_own.wait()
    everyone = conv_t.at[pl.ds(0, N_DEV - 1)]
    remote(everyone, everyone, act_send, act_recv, right).wait()
    act_copy = pltpu.make_async_copy(act_v, act_out.at[0], local_sem.at[7])
    act_copy.start()
    act_copy.wait()
    for copy in copies[4:]:
        copy.wait()


def local(fine_input, weights, norm_gain, norm_shift, cotangent):
    any_space = pl.BlockSpec(memory_space=pl.ANY)
    vmem = pl.BlockSpec(memory_space=pltpu.VMEM)
    smem = pl.BlockSpec(memory_space=pltpu.SMEM)
    dma = pltpu.SemaphoreType.DMA
    activated, grad_input, grad_weights, grad_gain, grad_shift = pl.pallas_call(
        kernel,
        out_shape=(
            jax.ShapeDtypeStruct((1, 32, 64, 128), F32),
            jax.ShapeDtypeStruct((CI, 4, 16, 256), F32),
            jax.ShapeDtypeStruct((27, CO, CI), F32),
            jax.ShapeDtypeStruct((1, 1), F32),
            jax.ShapeDtypeStruct((1, 1), F32),
        ),
        in_specs=[any_space, any_space, smem, smem, any_space],
        out_specs=(any_space, any_space, vmem, vmem, vmem),
        scratch_shapes=[
            pltpu.VMEM((4, CI, 16, 256), F32),
            pltpu.VMEM((27, CO, CI), F32),
            pltpu.VMEM((CO, 2, 8, 128), F32),
            pltpu.VMEM((2, 768, 1024), BF16),
            pltpu.VMEM((2, 768, 1024), BF16),
            pltpu.VMEM((1024, 128), F32),
            pltpu.VMEM((1024, 128), F32),
            pltpu.VMEM((256, 576), BF16),
            pltpu.VMEM((512, 576), BF16),
            pltpu.VMEM((1152, 768), BF16),
            pltpu.VMEM((3, CO, 1152), F32),
            pltpu.VMEM((CO, 2, 8, 128), F32),
            pltpu.VMEM((CO, 1024), F32),
            pltpu.VMEM((2, CO, 128), F32),
            pltpu.VMEM((CO, 128), F32),
            pltpu.VMEM((3, CO, 1152), F32),
            pltpu.VMEM((3, 256, 1152), BF16),
            pltpu.VMEM((3, 768, 1152), BF16),
            pltpu.VMEM((4, 2, 128, 1024), F32),
            pltpu.VMEM((2, 2, 1024, 128), F32),
            pltpu.VMEM((32, 64, 128), F32),
            pltpu.VMEM((4, 8, 128), F32),
            pltpu.VMEM((2, GX, 8, 128), F32),
            pltpu.VMEM((2, GY, 8, 128), F32),
            pltpu.VMEM((27 * CI, 128), F32),
            pltpu.VMEM((N_DEV, 16, 128), F32),
            pltpu.VMEM((27 * CI, 128), F32),
            dma((8,)),
            dma((2, 2)),
            dma,
            dma,
            dma((3,)),
            dma((3,)),
            dma((4,)),
            dma((4,)),
            dma,
            dma,
            dma((3,)),
            dma((3,)),
            dma,
            dma,
            dma,
            dma,
        ],
        compiler_params=pltpu.CompilerParams(
            collective_id=0, has_side_effects=True, vmem_limit_bytes=60 << 20
        ),
    )(fine_input, weights, norm_gain, norm_shift, cotangent)
    return activated, grad_input, grad_weights, grad_gain.reshape(1), grad_shift.reshape(1)


def solution(mesh):
    placed = (
        P(None, "gx", "gy", None),
        P(),
        P(("gx", "gy")),
        P(("gx", "gy")),
        P(("gx", "gy"), None, None, None),
    )
    return jax.shard_map(
        local,
        mesh=mesh,
        in_specs=placed,
        out_specs=(
            P(("gx", "gy"), None, None, None),
            P(None, "gx", "gy", None),
            P(),
            P(("gx", "gy")),
            P(("gx", "gy")),
        ),
        check_vma=False,
    )
```

time: 483 us -> 147 us (0.30); the launches traced: 477 us -> 146 us
  waiting for transfers between devices: 190 us -> 0 us
  matrix products: 142 us -> 0 us
  Pallas kernels: 0 us -> 127 us
  local copies, waits for them, and re-layouts: 79.5 us -> 13.1 us
  starting transfers between devices: 32.6 us -> 0 us
  between operations: 22.4 us -> 5.45 us
  other arithmetic: 10.4 us -> 0 us
    dot_general x81 -> x0, matrix products: 142 us -> none  [the longest x27 53.9 us: local(): jnp.einsum('oc,cxyz->oxyz', weights[(off_x * 3 + off_y) * 3 + off_z], fin...]
    psum x1 -> x0, waiting for transfers between devices: 134 us -> none  [local(): raw_w = lax.psum(jnp.stack(term_list), ('gx', 'gy'))]
    pallas_call x0 -> x1, Pallas kernels: none -> 127 us  [local(): pl.pallas_call(kernel, out_shape=(jax.ShapeDtypeStruct((1, 32, 64, 128),...]
    reshape x2 -> x0, local copies, waits for them, and re-layouts: 31.7 us -> none  [the longest x1 19.4 us: local(): extended.reshape(in_ch, coarse_x + 1, 2, coarse_y + 1, 2, coarse_z, 2)]
    all_to_all x2 -> x0, waiting for transfers between devices: 30.2 us -> none  [the longest x1 18.2 us: local(): lax.all_to_all(conv_local, ('gx', 'gy'), split_axis=0, concat_axis=1, til...]
    ppermute x4 -> x0, waiting for transfers between devices: 25.2 us -> none  [passed_along(): return lax.ppermute(block, axis, route)]
    all_to_all x2 -> x0, starting transfers between devices: 20.1 us -> none  [the longest x1 16.2 us: local(): lax.all_to_all(conv_local, ('gx', 'gy'), split_axis=0, concat_axis=1, til...]
    ppermute x4 -> x0, starting transfers between devices: 12 us -> none  [passed_along(): return lax.ppermute(block, axis, route)]
  transfers between devices with their start and end apart: 7 -> 0, of which waited for: 6 -> 0; matrix products, arithmetic and copies ran while one was open for 3% -> 0% of each run, Pallas kernels for 0% -> 0%
where the time goes in v1:
time: 147 us; the launch traced here: 146 us
  Pallas kernels  127 us (86%)
  local copies, waits for them, and re-layouts  13.1 us (9%)
  between operations  5.45 us (4%)
    pallas_call x1, Pallas kernels, local(): pl.pallas_call(kernel, out_shape=(jax.ShapeDtypeStruct((1, 32, 64, 128),...  127 us
    unnamed x4, local copies, waits for them, and re-layouts  13.1 us

profile of v1, /device:TPU:1, one launch (start us, length us, event | category | flops | bytes accessed | tf_op | source)
XLA Modules:
  0.0 145.7 jit_solution(6550157497269112438)
XLA Ops:
  1.9 2.9 %copy.10.wts = f32[27,128,64]{2,1,0:T(8,128)} copy(f32[27,128,64]{1,2,0:T(8,128)} %param.6) | data formatting | bytes 1769472 | tf_op args[1]
  4.8 127.1 %shard_map.92 = (f32[1,32,64,128]{3,2,1,0:T(8,128)}, f32[64,4,16,256]{3,2,1,0:T(8,128)}, f32[27,128,64]{2,1,0:T(8,128)}, f32[1,1]{1,0:T(1,128)}, f32[1,1]{1,0:T(1,128)}) custom-call(f32[64,4,16,256]{3,2,1,0:T(8,128)} %fine.1, f32[27,128,64]{2,1,0:T(8,128)} %copy.10.wts, f32[1]{0:T(128)S(6)} %copy.16.gain, f32[1]{0:T(128)S(6)} %copy.17.shift, ...), custom_call_target="tpu_custom_call" | custom-call | tf_op jit(solution)/shard_map/pallas_call | solution.py:483
  131.9 2.9 %copy.11 = f32[27,128,64]{1,2,0:T(8,128)} copy(f32[27,128,64]{2,1,0:T(8,128)} %get-tuple-element.17) | data formatting | bytes 1769472
  134.8 2.3 %copy.18 = f32[1,32,64,128]{3,2,1,0:T(8,128)} copy(f32[1,32,64,128]{3,2,1,0:T(8,128)} %get-tuple-element.25) | data formatting | bytes 2097152
  137.1 5.0 %copy.19 = f32[64,4,16,256]{3,2,1,0:T(8,128)} copy(f32[64,4,16,256]{3,2,1,0:T(8,128)} %get-tuple-element.26) | data formatting | bytes 8388608

commit v2 on v1

v2 whole, which is shorter than its diff:
```python
import functools
import math

import jax
import jax.numpy as jnp
from jax import lax
from jax.experimental import pallas as pl
from jax.experimental.pallas import tpu as pltpu
from jax.sharding import PartitionSpec as P

MESH = pl.DeviceIdType.MESH
F32 = jnp.float32
BF16 = jnp.bfloat16
GX, GY, N_DEV = 16, 8, 128
CI, CO = 64, 128
CELLS = 32 * 64 * 128
OWN_CELLS = CELLS // N_DEV
RESCALE = 1.0 / math.sqrt(CELLS)
EPSILON = 1e-5
N_CHIP = N_DEV // 2
HALF = 27 * CI // 2
OWNERS = HALF // 16
ACT_CUTS = ((1, 32), (32, 64), (64, 96), (96, 128))


def dot(a, b):
    return jnp.dot(a, b, preferred_element_type=F32)


def dot_nt(a, b):
    return lax.dot_general(a, b, (((1,), (1,)), ((), ())), preferred_element_type=F32)


def high_low(value):
    high = value.astype(BF16)
    return high, (value - high.astype(F32)).astype(BF16)


def rows_to_columns(rows):
    return jnp.concatenate([rows, jnp.zeros((120, 128), F32)], axis=0).T


def kernel(
    fine, wts, gain, shift, cot, act_out, gin_out, gw_out, gg_out, gs_out,
    fine_v, w_v, cot_v, x_hi, x_lo, even_t, odd_t, wf_e, wf_o, wb, conv, conv_t, rim_out, rim_x, rim_y, rim_c,
    g_f, g_w, g_i, o_acc, out_v, act_v, stat, stat_x, stat_y, wg, wg_pair, wg_half, wg_in, wg_all,
    local_sem, out_sem, cot_send, cot_recv, rim_send, rim_recv, stat_send, stat_recv,
    act_send, act_recv, g_send, g_recv, wr_send, wr_recv, wa_send, wa_recv, pair_send, pair_recv,
):
    gx, gy = lax.axis_index("gx"), lax.axis_index("gy")
    me = gx * GY + gy

    def at(lin):
        return (lin // GY, lax.rem(lin, GY))

    def remote(src, dst, send, recv, device):
        return pltpu.make_async_remote_copy(
            src_ref=src, dst_ref=dst, send_sem=send, recv_sem=recv,
            device_id=device, device_id_type=MESH,
        )

    fine_in = [
        pltpu.make_async_copy(fine.at[:, x], fine_v.at[x], local_sem.at[x]) for x in (3, 2, 1, 0)
    ]
    for copy in fine_in:
        copy.start()
    w_in = pltpu.make_async_copy(wts, w_v, local_sem.at[4])
    w_in.start()
    my_cells = (pl.ds(2 * gx, 2), pl.ds(pl.multiple_of(8 * gy, 8), 8), slice(None))
    cot_own = pltpu.make_async_copy(cot.at[(0,) + my_cells], cot_v.at[me], local_sem.at[5])
    cot_own.start()

    barrier = pltpu.get_barrier_semaphore()

    def greet(k, carry):
        pl.semaphore_signal(
            barrier, inc=1, device_id=at(lax.rem(me + k, N_DEV)), device_id_type=MESH
        )
        return carry

    lax.fori_loop(1, N_DEV, greet, 0)

    row = lax.broadcasted_iota(jnp.int32, (256, 256), 0)
    col = lax.broadcasted_iota(jnp.int32, (256, 256), 1)
    split = jnp.where(
        row == jnp.where(col < 128, 2 * col, 2 * (col - 128) + 1), 1.0, 0.0
    ).astype(BF16)
    merge = jnp.where(
        col == jnp.where(row < 128, 2 * row, 2 * (row - 128) + 1), 1.0, 0.0
    ).astype(BF16)
    lane = lax.broadcasted_iota(jnp.int32, (64, 128), 1)

    w_in.wait()
    for b in range(3):
        flat = jnp.concatenate([w_v[(a * 3 + b) * 3 + c] for a in range(3) for c in range(3)], axis=0)
        high, low = high_low(flat.T)
        if b == 1:
            wf_e[0:128], wf_e[128:256] = high, low
        else:
            at_row = 0 if b == 2 else 128
            wf_o[at_row : at_row + 128] = high
            wf_o[256 + at_row : 384 + at_row] = low

    def send_cot(k, carry):
        to = lax.rem(me + k, N_DEV)
        tx, ty = at(to)
        src = cot.at[0, pl.ds(2 * tx, 2), pl.ds(pl.multiple_of(8 * ty, 8), 8), :]
        remote(src, cot_v.at[me], cot_send, cot_recv, (tx, ty)).start()
        return carry

    right = (lax.rem(gx + 1, GX), gy)
    up = (gx, lax.rem(gy + 1, GY))
    right_up = (lax.rem(gx + 1, GX), lax.rem(gy + 1, GY))
    left = (lax.rem(gx + GX - 1, GX), gy)
    down = (gx, lax.rem(gy + GY - 1, GY))
    left_down = (lax.rem(gx + GX - 1, GX), lax.rem(gy + GY - 1, GY))

    def exchange_start(k, stage):
        index, parts = 2 * k + stage, (stat_x, stat_y)[stage]
        place, count = ((gx, GX), (gy, GY))[stage]

        def send(d, carry):
            to = lax.rem(place + d, count)
            device = ((to, gy), (gx, to))[stage]
            remote(stat.at[index], parts.at[k, place], stat_send.at[index], stat_recv.at[index], device).start()
            return carry

        lax.fori_loop(1, count, send, 0)
        parts[k, pl.ds(place, 1)] = stat[pl.ds(index, 1)]

    def exchange_wait(k, stage):
        index, parts = 2 * k + stage, (stat_x, stat_y)[stage]
        everyone = parts.at[k, pl.ds(0, (GX, GY)[stage] - 1)]
        remote(everyone, everyone, stat_send.at[index], stat_recv.at[index], (right, up)[stage]).wait()

    def split_slab(x):
        high, low = high_low(fine_v[x].reshape(CI * 16, 256))
        for part, dst in ((high, x_hi), (low, x_lo)):
            both = dot(part, split)
            even_t[...] = both[:, :128]
            odd_t[...] = both[:, 128:]

            for y in range(16):
                half, lanes = y % 2, slice(y // 2 * 128, y // 2 * 128 + 128)
                even = even_t[pl.ds(y, CI, stride=16), :]
                odd = odd_t[pl.ds(y, CI, stride=16), :]
                before = jnp.where(lane == 0, 0.0, pltpu.roll(odd, 1, 1))
                dst[half, x * 192 : x * 192 + 64, lanes] = before.astype(BF16)
                dst[half, x * 192 + 64 : x * 192 + 128, lanes] = even.astype(BF16)
                dst[half, x * 192 + 128 : x * 192 + 192, lanes] = odd.astype(BF16)

    def operands(mx):
        x0, x1 = ((0, 2), (1, 4), (3, 4))[mx]
        a0 = (1, 0, 0)[mx]
        depth = (x1 - x0) * 192
        return slice(x0 * 192, x1 * 192), slice(a0 * 192, a0 * 192 + depth)

    def forward_rim(mx):
        rows, cols = operands(mx)
        value = dot(wf_o[:, cols], x_hi[1, rows, 896:1024])
        return value[128:256] + value[384:512] + dot(wf_o[128:256, cols], x_lo[1, rows, 896:1024])

    def forward(mx):
        rows, cols = operands(mx)
        conv[mx, :, 0:128] = jnp.zeros((CO, 128), F32)

        def chunk(n, carry):
            here = pl.ds(pl.multiple_of(n * 256, 256), 256)
            e_hi, e_lo = x_hi[0, rows, here], x_lo[0, rows, here]
            o_hi, o_lo = x_hi[1, rows, here], x_lo[1, rows, here]
            e = dot(wf_e[:, cols], e_hi)
            e = e[:128] + e[128:] + dot(wf_e[0:128, cols], e_lo)
            o = dot(wf_o[:, cols], o_hi)
            o = o[:256] + o[256:] + dot(wf_o[0:256, cols], o_lo)
            e = e + o[:128]
            conv[mx, :, pl.ds(pl.multiple_of(n * 256, 256), 128)] += e[:, :128]
            conv[mx, :, pl.ds(pl.multiple_of(n * 256 + 128, 128), 128)] = e[:, 128:] + o[128:, :128]
            conv[mx, :, pl.ds(pl.multiple_of(n * 256 + 256, 256), 128)] = o[128:, 128:]
            return carry

        lax.fori_loop(0, 4, chunk, 0)

    fine_in[0].wait()
    split_slab(3)
    forward(2)
    pl.semaphore_wait(barrier, N_DEV - 1)
    rims = [
        remote(conv.at[2, :, pl.ds(0, 1024)], rim_x, rim_send.at[0], rim_recv.at[0], right),
        remote(conv.at[2, :, pl.ds(1024, 128)], rim_c, rim_send.at[1], rim_recv.at[1], right_up),
    ]
    rims[0].start()
    rims[1].start()
    one_row = lax.broadcasted_iota(jnp.int32, (1, 128), 1)
    mine = one_row == me
    stat[4] = jnp.concatenate([jnp.where(mine, gain[0], 0.0), jnp.where(mine, shift[0], 0.0)], axis=0)
    exchange_start(2, 0)
    lax.fori_loop(1, N_DEV, send_cot, 0)
    for i, x in ((1, 2), (2, 1), (3, 0)):
        fine_in[i].wait()
        split_slab(x)
    for mx in range(2):
        rim_out[mx] = forward_rim(mx)
    rims.append(remote(rim_out, rim_y, rim_send.at[2], rim_recv.at[2], up))
    rims[2].start()
    forward(1)
    forward(0)

    for tap in range(9):
        turned = [w_v[tap * 3 + c] for c in range(3)]
        for half, (now, later) in enumerate(((turned[1], None), (turned[2], turned[0]))):
            rows = slice(tap * 128 + half * 64, tap * 128 + half * 64 + 64)
            for k, block in enumerate((now, later)):
                if block is None:
                    high = low = jnp.zeros((64, 128), BF16)
                else:
                    high, low = high_low(block)
                wb[rows, k * 128 : k * 128 + 128] = high
                wb[rows, 256 + k * 128 : 384 + k * 128] = high
                wb[rows, 512 + k * 128 : 640 + k * 128] = low

    exchange_wait(2, 0)
    stat[5] = jnp.sum(stat_x[2], axis=0)
    exchange_start(2, 1)
    for copy in rims:
        copy.wait()
    has_left = jnp.where(gx > 0, 1.0, 0.0)
    has_down = jnp.where(gy > 0, 1.0, 0.0)
    conv[0, :, 0:1024] += rim_x[...] * has_left
    conv[0, :, 0:128] += rim_c[...] * (has_left * has_down)
    for mx in range(2):
        conv[mx, :, 0:128] += rim_y[mx] * has_down

    conv_rows = conv_t.reshape(CO * 16, 128)
    own = [conv[mx, :, 128 * my : 128 * my + 128] for mx in range(2) for my in range(8)]
    average = jnp.sum(functools.reduce(jnp.add, own), axis=1, keepdims=True) * (1.0 / OWN_CELLS)
    spread = jnp.sum(
        functools.reduce(jnp.add, [(v - average) * (v - average) for v in own]), axis=1, keepdims=True
    )
    wide = lax.broadcasted_iota(jnp.int32, (128, 128), 1)
    stat[0] = jnp.where(wide == 0, average, jnp.where(wide == 1, spread, 0.0)).T[0:2]
    for row_of in range(16):
        conv_rows[pl.ds(row_of, 128, stride=16), :] = conv[row_of // 8, :, row_of % 8 * 128 : row_of % 8 * 128 + 128]
    act_own = pltpu.make_async_copy(conv_t.at[me], act_v.at[my_cells], local_sem.at[6])
    act_own.start()

    def send_act(k, carry):
        to = lax.rem(me + k, N_DEV)
        remote(conv_t.at[to], act_v.at[my_cells], act_send, act_recv, at(to)).start()
        return carry

    def combine_moments(parts, cells):
        count = parts.shape[0]
        total = jnp.sum(parts, axis=0)
        mean = total[0:1] * (1.0 / count)
        away = parts[:, 0:1] - mean[None]
        return jnp.concatenate([mean, total[1:2] + cells * jnp.sum(away * away, axis=0)], axis=0)

    exchange_start(0, 0)
    lax.fori_loop(*ACT_CUTS[0], send_act, 0)
    exchange_wait(0, 0)
    stat[1] = combine_moments(stat_x[0], OWN_CELLS)
    exchange_start(0, 1)
    lax.fori_loop(*ACT_CUTS[1], send_act, 0)
    exchange_wait(0, 1)
    moments = combine_moments(stat_y[0], OWN_CELLS * GX)
    exchange_wait(2, 1)
    scales = jnp.sum(stat_y[2], axis=0)
    inv_row = 1.0 / jnp.sqrt(moments[1:2] * (1.0 / CELLS) + EPSILON)
    rows = jnp.concatenate([moments[0:1], inv_row, scales, jnp.zeros((4, 128), F32)], axis=0)
    own_average, own_inv_std = (
        jnp.sum(jnp.where(mine, r, 0.0), axis=1, keepdims=True) for r in (moments[0:1], inv_row)
    )
    columns = rows_to_columns(rows)
    average, inv_std = columns[:, 0:1], columns[:, 1:2]
    gain_col, shift_col = columns[:, 2:3], columns[:, 3:4]

    cot_own.wait()
    everyone = cot_v.at[pl.ds(0, N_DEV - 1)]
    remote(everyone, everyone, cot_send, cot_recv, right).wait()
    cot_rows = cot_v.reshape(CO * 16, 128)
    sums = jnp.zeros((128, 128), F32), jnp.zeros((128, 128), F32)
    for mx in range(2):

        def one_cell(my, carry, mx=mx):
            s0, s1 = carry
            lanes = pl.ds(pl.multiple_of(my * 128, 128), 128)
            value = conv[mx, :, lanes]
            normed = (value - average) * inv_std
            pre = gain_col * normed + shift_col
            sig = 1.0 / (1.0 + jnp.exp(-pre))
            grad = cot_rows[pl.ds(mx * 8 + my, 128, stride=16), :] * sig * (1.0 + pre * (1.0 - sig))
            g_f[mx, :, lanes] = grad
            return s0 + grad, s1 + grad * normed

        sums = lax.fori_loop(0, 8, one_cell, sums, unroll=4)
    stat[2] = jnp.concatenate([jnp.sum(s.T, axis=0, keepdims=True) for s in sums], axis=0)
    exchange_start(1, 0)
    lax.fori_loop(*ACT_CUTS[2], send_act, 0)
    exchange_wait(1, 0)
    stat[3] = jnp.sum(stat_x[1], axis=0)
    exchange_start(1, 1)
    lax.fori_loop(*ACT_CUTS[3], send_act, 0)
    exchange_wait(1, 1)
    totals = jnp.sum(stat_y[1], axis=0)
    gs_out[...] = jnp.sum(jnp.where(mine, totals[0:1], 0.0), axis=1, keepdims=True) * RESCALE
    gg_out[...] = jnp.sum(jnp.where(mine, totals[1:2], 0.0), axis=1, keepdims=True) * RESCALE
    columns2 = rows_to_columns(jnp.concatenate([totals, jnp.zeros((6, 128), F32)], axis=0))
    mean_g = gain_col * columns2[:, 0:1] * (1.0 / CELLS)
    mean_gn = gain_col * columns2[:, 1:2] * (1.0 / CELLS)

    def place(mx, lanes, value):
        high, low = high_low(value)
        g_w[mx, 0:128, lanes] = high
        g_w[mx, 128:256, lanes] = low
        g_i[mx, 0:128, lanes] = high
        g_i[mx, 256:384, lanes] = low
        g_i[mx, 512:640, lanes] = high
        moved = jnp.where(wide == 127, 0.0, pltpu.roll(value, 127, 1))
        high, low = high_low(moved)
        g_i[mx, 128:256, lanes] = high
        g_i[mx, 384:512, lanes] = low
        g_i[mx, 640:768, lanes] = high

    def finish_row(mx):
        def finish(my, carry):
            lanes = pl.ds(pl.multiple_of(my * 128, 128), 128)
            normed = (conv[mx, :, lanes] - average) * inv_std
            value = inv_std * (gain_col * g_f[mx, :, lanes] - mean_g - normed * mean_gn)
            g_f[mx, :, lanes] = value
            place(mx, lanes, value)
            return carry

        lax.fori_loop(0, 8, finish, 0, unroll=4)

    finish_row(0)
    g_rims = [
        remote(g_f.at[0, :, pl.ds(0, 1024)], g_f.at[2, :, pl.ds(0, 1024)], g_send.at[0], g_recv.at[0], left),
        remote(g_f.at[pl.ds(0, 2), :, pl.ds(0, 128)], g_f.at[pl.ds(0, 2), :, pl.ds(1024, 128)], g_send.at[1], g_recv.at[1], down),
        remote(g_f.at[0, :, pl.ds(0, 128)], g_f.at[2, :, pl.ds(1024, 128)], g_send.at[2], g_recv.at[2], left_down),
    ]
    g_rims[0].start()
    g_rims[2].start()
    finish_row(1)
    g_rims[1].start()

    def weight_terms(mx, b, x_lanes, g_lanes, fresh=False):
        half = 0 if b == 1 else 1
        rows, cols = operands(mx)
        g_here = g_w[mx, :, g_lanes]
        both = dot_nt(x_hi[half, rows, x_lanes], g_here)
        value = both[:, :128] + both[:, 128:] + dot_nt(x_lo[half, rows, x_lanes], g_here[:128])
        target = slice(b * 576 + cols.start, b * 576 + cols.stop)
        if fresh:
            wg[target] = value
        else:
            wg[target] += value

    def add_to(x, half, lanes, value, fresh):
        if fresh:
            o_acc[x, half, :, lanes] = value
        else:
            o_acc[x, half, :, lanes] += value

    def input_terms(mx):
        taps = [a for a in range(3) if 0 <= 2 * mx - 1 + a <= 3]
        top, bottom = taps[0] * 384, taps[-1] * 384 + 384

        def chunk(n, carry):
            here = pl.ds(pl.multiple_of(n * 256, 256), 256)
            first = pl.ds(pl.multiple_of(n * 256, 256), 128)
            second = pl.ds(pl.multiple_of(n * 256 + 128, 128), 128)
            terms = dot(wb[top:bottom, :], g_i[mx, :, here])
            for a in taps:
                x = 2 * mx - 1 + a
                block = terms[a * 384 - top : a * 384 - top + 384]
                add_to(x, 0, here, block[128:256], a > 0)
                add_to(x, 1, first, block[256:384, :128] + block[0:128, 128:], a > 0)
                add_to(x, 1, second, block[256:384, 128:], a > 0)

                @pl.when(n > 0)
                def _(x=x, block=block):
                    before = pl.ds(pl.multiple_of(n * 256 - 128, 128), 128)
                    o_acc[x, 1, :, before] += block[0:128, :128]

            return carry

        lax.fori_loop(0, 4, chunk, 0)

    def input_terms_rim(mx):
        for a in range(3):
            x = 2 * mx - 1 + a
            if 0 <= x <= 3:
                value = dot(wb[a * 384 : a * 384 + 128, :], g_i[mx, :, 1024:1152])
                o_acc[x, 1, :, 896:1024] += value

    everything = slice(0, 1024)
    for mx in (1, 0):
        weight_terms(mx, 0, slice(0, 896), slice(128, 1024), mx == 1)
        weight_terms(mx, 1, everything, everything, mx == 1)
        weight_terms(mx, 2, everything, everything, mx == 1)
    input_terms(0)
    input_terms(1)
    for copy in g_rims:
        copy.wait()
    has_right = jnp.where(gx < GX - 1, 1.0, 0.0)
    has_up = jnp.where(gy < GY - 1, 1.0, 0.0)

    def finish_x(my, carry):
        lanes = pl.ds(pl.multiple_of(my * 128, 128), 128)
        place(2, lanes, g_f[2, :, lanes] * has_right)
        return carry

    lax.fori_loop(0, 8, finish_x, 0, unroll=4)
    for mx, there in ((0, has_up), (1, has_up), (2, has_up * has_right)):
        place(mx, slice(1024, 1152), g_f[mx, :, 1024:1152] * there)
    for mx in range(2):
        weight_terms(mx, 0, slice(896, 1024), slice(1024, 1152))
    weight_terms(2, 0, everything, slice(128, 1152))
    weight_terms(2, 1, everything, everything)
    weight_terms(2, 2, everything, everything)

    core, chip = lax.rem(gx, 2), (gx // 2) * GY + gy
    pair_device = (gx + 1 - 2 * core, gy)
    other_half = pl.ds(pl.multiple_of((1 - core) * HALF, HALF), HALF)
    own_half = pl.ds(pl.multiple_of(core * HALF, HALF), HALF)
    pair = remote(wg.at[other_half], wg_pair, pair_send.at[0], pair_recv.at[0], pair_device)
    pair.start()

    def chip_device(index):
        return (2 * (index // GY) + core, lax.rem(index, GY))

    def slice_of(index):
        return pl.ds(pl.multiple_of(index * 16, 16), 16)

    pair.wait()
    wg_half[...] = wg[own_half] + wg_pair[...]

    def send_part(k, carry):
        to = lax.rem(chip + k, N_CHIP)

        @pl.when(to < OWNERS)
        def _():
            remote(wg_half.at[slice_of(to)], wg_in.at[chip], wr_send, wr_recv, chip_device(to)).start()

        return carry

    lax.fori_loop(1, N_CHIP, send_part, 0)
    input_terms(2)
    for mx in range(3):
        input_terms_rim(mx)
    copies = []
    for x in range(4):
        slot = x % 2
        if x >= 2:
            for copy in copies[2 * (x - 2) : 2 * (x - 2) + 2]:
                copy.wait()
        for half in range(2):
            blocks = [
                jnp.concatenate(
                    [o_acc[x, half, 0:64, 128 * my : 128 * my + 128], o_acc[x, half, 64:128, 128 * my : 128 * my + 128]],
                    axis=1,
                )
                for my in range(8)
            ]
            high, low = high_low(jnp.concatenate(blocks, axis=0))
            merged = dot(high, merge) + dot(low, merge)
            for my in range(8):
                for z in range(2):
                    out_v[slot, z, pl.ds(2 * my + half, 64, stride=16), :] = merged[
                        64 * my : 64 * my + 64, 128 * z : 128 * z + 128
                    ]
        for z in range(2):
            copy = pltpu.make_async_copy(
                out_v.at[slot, z].reshape(CI, 16, 128),
                gin_out.at[:, x, :, pl.ds(128 * z, 128)],
                out_sem.at[slot, z],
            )
            copy.start()
            copies.append(copy)

    @pl.when(chip < OWNERS)
    def _():
        wg_in[pl.ds(chip, 1)] = wg_half[slice_of(chip)][None]
        everyone = wg_in.at[pl.ds(0, N_CHIP - 1)]
        remote(everyone, everyone, wr_send, wr_recv, right).wait_recv()
        own_slice = pl.ds(pl.multiple_of(core * HALF + chip * 16, 16), 16)
        wg_all[own_slice] = jnp.sum(wg_in[...], axis=0) * RESCALE

        def send_slice(k, carry):
            to = lax.rem(chip + k, N_CHIP)
            src = wg_all.at[own_slice]
            remote(src, src, wa_send, wa_recv, chip_device(to)).start()
            return carry

        lax.fori_loop(1, N_CHIP, send_slice, 0)
        some = wg_half.at[pl.ds(0, 16 * (OWNERS - 1))]
        remote(some, some, wr_send, wr_recv, right).wait_send()
        remote(everyone, everyone, wa_send, wa_recv, right).wait_send()
        some = wg_all.at[pl.ds(0, 16 * (OWNERS - 1))]
        remote(some, some, wa_send, wa_recv, right).wait_recv()

    @pl.when(chip >= OWNERS)
    def _():
        remote(wg_half, wg_half, wr_send, wr_recv, right).wait_send()
        some = wg_all.at[pl.ds(0, HALF)]
        remote(some, some, wa_send, wa_recv, right).wait_recv()

    done = wg_all.at[own_half]
    pair = remote(done, done, pair_send.at[1], pair_recv.at[1], pair_device)
    pair.start()
    act_own.wait()
    everyone = conv_t.at[pl.ds(0, N_DEV - 1)]
    remote(everyone, everyone, act_send, act_recv, right).wait()
    own_scale = own_inv_std * gain[0]

    def activate(i, carry):
        here = pl.ds(i * 4, 4)
        pre = (act_v[here] - own_average[None]) * own_scale[None] + shift[0]
        act_v[here] = pre / (1.0 + jnp.exp(-pre))
        return carry

    lax.fori_loop(0, 8, activate, 0)
    act_copy = pltpu.make_async_copy(act_v, act_out, local_sem.at[7])
    act_copy.start()
    pair.wait()
    for a in range(3):
        for b in range(3):
            rows = slice((b * 3 + a) * 192, (b * 3 + a) * 192 + 192)
            gw_out[(a * 3 + b) * 3 : (a * 3 + b) * 3 + 3] = wg_all[rows].reshape(3, CI, CO)
    act_copy.wait()
    for copy in copies[4:]:
        copy.wait()


def hand_over(*refs):
    sources, targets, buffers, sem = refs[:3], refs[3:6], refs[6:9], refs[9]
    reads, writes = [], []
    for source, target, buffer, pieces in zip(sources, targets, buffers, (2, 8, 1)):
        size = source.shape[0] // pieces
        for piece in range(pieces):
            here = pl.ds(piece * size, size)
            k = len(reads)
            reads.append(pltpu.make_async_copy(source.at[here], buffer.at[here], sem.at[0, k]))
            writes.append(pltpu.make_async_copy(buffer.at[here], target.at[here], sem.at[1, k]))
    for read in reads:
        read.start()
    for read, write in zip(reads, writes):
        read.wait()
        write.start()
    for write in writes:
        write.wait()


def local(fine_input, weights, norm_gain, norm_shift, cotangent):
    any_space = pl.BlockSpec(memory_space=pl.ANY)
    vmem = pl.BlockSpec(memory_space=pltpu.VMEM)
    smem = pl.BlockSpec(memory_space=pltpu.SMEM)
    dma = pltpu.SemaphoreType.DMA
    activated, grad_input, grad_weights, grad_gain, grad_shift = pl.pallas_call(
        kernel,
        out_shape=(
            jax.ShapeDtypeStruct((32, 64, 128), F32),
            jax.ShapeDtypeStruct((CI, 4, 16, 256), F32),
            jax.ShapeDtypeStruct((27, CI, CO), F32),
            jax.ShapeDtypeStruct((1, 1), F32),
            jax.ShapeDtypeStruct((1, 1), F32),
        ),
        in_specs=[any_space, any_space, smem, smem, any_space],
        out_specs=(any_space, any_space, vmem, vmem, vmem),
        scratch_shapes=[
            pltpu.VMEM((4, CI, 16, 256), F32),
            pltpu.VMEM((27, CI, CO), F32),
            pltpu.VMEM((CO, 2, 8, 128), F32),
            pltpu.VMEM((2, 768, 1024), BF16),
            pltpu.VMEM((2, 768, 1024), BF16),
            pltpu.VMEM((1024, 128), F32),
            pltpu.VMEM((1024, 128), F32),
            pltpu.VMEM((256, 576), BF16),
            pltpu.VMEM((512, 576), BF16),
            pltpu.VMEM((1152, 768), BF16),
            pltpu.VMEM((3, CO, 1152), F32),
            pltpu.VMEM((CO, 2, 8, 128), F32),
            pltpu.VMEM((2, CO, 128), F32),
            pltpu.VMEM((CO, 1024), F32),
            pltpu.VMEM((2, CO, 128), F32),
            pltpu.VMEM((CO, 128), F32),
            pltpu.VMEM((3, CO, 1152), F32),
            pltpu.VMEM((3, 256, 1152), BF16),
            pltpu.VMEM((3, 768, 1152), BF16),
            pltpu.VMEM((4, 2, 128, 1024), F32),
            pltpu.VMEM((2, 2, 1024, 128), F32),
            pltpu.VMEM((32, 64, 128), F32),
            pltpu.VMEM((6, 2, 128), F32),
            pltpu.VMEM((3, GX, 2, 128), F32),
            pltpu.VMEM((3, GY, 2, 128), F32),
            pltpu.VMEM((27 * CI, 128), F32),
            pltpu.VMEM((HALF, 128), F32),
            pltpu.VMEM((HALF, 128), F32),
            pltpu.VMEM((N_CHIP, 16, 128), F32),
            pltpu.VMEM((27 * CI, 128), F32),
            dma((8,)),
            dma((2, 2)),
            dma,
            dma,
            dma((3,)),
            dma((3,)),
            dma((6,)),
            dma((6,)),
            dma,
            dma,
            dma((3,)),
            dma((3,)),
            dma,
            dma,
            dma,
            dma,
            dma((2,)),
            dma((2,)),
        ],
        compiler_params=pltpu.CompilerParams(
            collective_id=0, has_side_effects=True, vmem_limit_bytes=60 << 20
        ),
    )(fine_input, weights.transpose(0, 2, 1), norm_gain, norm_shift, cotangent)
    activated, grad_input, grad_weights = pl.pallas_call(
        hand_over,
        out_shape=(
            jax.ShapeDtypeStruct((32, 64, 128), F32),
            jax.ShapeDtypeStruct((CI, 4, 16, 256), F32),
            jax.ShapeDtypeStruct((27, CI, CO), F32),
        ),
        in_specs=[any_space] * 3,
        out_specs=(any_space,) * 3,
        scratch_shapes=[
            pltpu.VMEM((32, 64, 128), F32),
            pltpu.VMEM((CI, 4, 16, 256), F32),
            pltpu.VMEM((27, CI, CO), F32),
            dma((2, 11)),
        ],
        compiler_params=pltpu.CompilerParams(vmem_limit_bytes=60 << 20),
    )(activated, grad_input, grad_weights)
    activated, grad_weights = activated[None], grad_weights.transpose(0, 2, 1)
    return activated, grad_input, grad_weights, grad_gain.reshape(1), grad_shift.reshape(1)


def solution(mesh):
    placed = (
        P(None, "gx", "gy", None),
        P(),
        P(("gx", "gy")),
        P(("gx", "gy")),
        P(("gx", "gy"), None, None, None),
    )
    return jax.shard_map(
        local,
        mesh=mesh,
        in_specs=placed,
        out_specs=(
            P(("gx", "gy"), None, None, None),
            P(None, "gx", "gy", None),
            P(),
            P(("gx", "gy")),
            P(("gx", "gy")),
        ),
        check_vma=False,
    )
```

time: 147 us -> 108 us (0.73)
  Pallas kernels: 127 us -> 103 us
  local copies, waits for them, and re-layouts: 13.1 us -> 0 us
    pallas_call x1 -> x2, Pallas kernels: 127 us -> 103 us  [the longest x1 97 us: local(): pl.pallas_call(kernel, out_shape=(jax.ShapeDtypeStruct((32, 64, 128), F32...]
    unnamed x4 -> x0, local copies, waits for them, and re-layouts: 13.1 us -> none
where the time goes in v2:
time: 108 us
  Pallas kernels  103 us (95%)
  between operations  5.37 us (5%)
    pallas_call x1, Pallas kernels, local(): pl.pallas_call(kernel, out_shape=(jax.ShapeDtypeStruct((32, 64, 128), F32...  97 us
    pallas_call x1, Pallas kernels, local(): pl.pallas_call(hand_over, out_shape=(jax.ShapeDtypeStruct((32, 64, 128),...  5.54 us

profile of v2, /device:TPU:1, one launch (start us, length us, event | category | flops | bytes accessed | tf_op | source)
XLA Modules:
  0.0 107.9 jit_solution(11173566178608896585)
XLA Ops:
  1.9 97.0 %shard_map.92 = (f32[32,64,128]{2,1,0:T(8,128)}, f32[64,4,16,256]{3,2,1,0:T(8,128)}, f32[27,64,128]{2,1,0:T(8,128)}, f32[1,1]{1,0:T(1,128)}, f32[1,1]{1,0:T(1,128)}) custom-call(f32[64,4,16,256]{3,2,1,0:T(8,128)} %fine.1, f32[27,64,128]{2,1,0:T(8,128)} %bitcast.5, f32[1]{0:T(128)S(6)} %copy.12.gain, f32[1]{0:T(128)S(6)} %copy.13.shift, f32[1,32,64,128]{3,2,1,0:T(8,128)} %cot.1), custom_call_target="tpu_custom_call" | custom-call | tf_op jit(solution)/shard_map/pallas_call | solution.py:559
  98.9 5.5 %shard_map.93 = (f32[32,64,128]{2,1,0:T(8,128)}, f32[64,4,16,256]{3,2,1,0:T(8,128)}, f32[27,64,128]{2,1,0:T(8,128)}) custom-call(f32[32,64,128]{2,1,0:T(8,128)} %get-tuple-element.13.refs_0_, f32[64,4,16,256]{3,2,1,0:T(8,128)} %get-tuple-element.14.refs_1_, f32[27,64,128]{2,1,0:T(8,128)} %get-tuple-element.15.refs_2_), custom_call_target="tpu_custom_call" | custom-call | tf_op jit(solution)/shard_map/pallas_call | solution.py:624

commit v3 on v2

v3 whole, which is shorter than its diff:
```python
import functools
import math

import jax
import jax.numpy as jnp
from jax import lax
from jax.experimental import pallas as pl
from jax.experimental.pallas import tpu as pltpu
from jax.sharding import PartitionSpec as P

MESH = pl.DeviceIdType.MESH
F32 = jnp.float32
BF16 = jnp.bfloat16
GX, GY, N_DEV = 16, 8, 128
CI, CO = 64, 128
CELLS = 32 * 64 * 128
RESCALE = 1.0 / math.sqrt(CELLS)
EPSILON = 1e-5
N_CHIP = N_DEV // 2
HALF = 27 * CI // 2
OWNERS = HALF // 16
FIRST = (16, 8, 0)
PARTS = ((0, 8), (8, 8), (16, 11))
GROUPS = ((0, 576), (1152, 288))
CUT = 36


def dot(a, b):
    return jnp.dot(a, b, preferred_element_type=F32)


def dot_nt(a, b):
    return lax.dot_general(a, b, (((1,), (1,)), ((), ())), preferred_element_type=F32)


def high_low(value):
    high = value.astype(BF16)
    return high, (value - high.astype(F32)).astype(BF16)


def rows_to_columns(rows):
    return jnp.concatenate([rows, jnp.zeros((120, 128), F32)], axis=0).T


def kernel(
    fine, wts, gain, shift, cot, act_out, gin_out, gw_out, gg_out, gs_out,
    fine_v, w_v, cot_v, x_hi, x_lo, even_t, odd_t, wf_e, wf_o, wb,
    conv, pair_x, cells_out, cells_in, whole, grad_out, grad_in, g_w, g_i, o_acc, out_v, act_v,
    wg, wg_pair, wg_half, wg_in, wg_all,
    local_sem, out_sem, conv_send, conv_recv, grad_send, grad_recv, wr_send, wr_recv, wa_send, wa_recv,
    pair_send, pair_recv,
):
    gx, gy = lax.axis_index("gx"), lax.axis_index("gy")
    me = gx * GY + gy
    core, chip = lax.rem(gx, 2), (gx // 2) * GY + gy
    pair_device = (gx + 1 - 2 * core, gy)
    right = (lax.rem(gx + 1, GX), gy)

    def at(lin):
        return (lin // GY, lax.rem(lin, GY))

    def remote(src, dst, send, recv, device):
        return pltpu.make_async_remote_copy(
            src_ref=src, dst_ref=dst, send_sem=send, recv_sem=recv,
            device_id=device, device_id_type=MESH,
        )

    fine_in = [
        pltpu.make_async_copy(fine.at[:, x], fine_v.at[x], local_sem.at[x]) for x in (3, 2, 1, 0)
    ]
    for copy in fine_in:
        copy.start()
    w_in = pltpu.make_async_copy(wts, w_v, local_sem.at[4])
    w_in.start()
    cot_in = pltpu.make_async_copy(cot.at[0], cot_v, local_sem.at[5])
    cot_in.start()

    barrier = pltpu.get_barrier_semaphore()

    def greet(k, carry):
        pl.semaphore_signal(
            barrier, inc=1, device_id=at(lax.rem(me + k, N_DEV)), device_id_type=MESH
        )
        return carry

    lax.fori_loop(1, N_DEV, greet, 0)

    row = lax.broadcasted_iota(jnp.int32, (256, 256), 0)
    col = lax.broadcasted_iota(jnp.int32, (256, 256), 1)
    split = jnp.where(
        row == jnp.where(col < 128, 2 * col, 2 * (col - 128) + 1), 1.0, 0.0
    ).astype(BF16)
    merge_z = jnp.where(
        col == jnp.where(row < 128, 2 * row, 2 * (row - 128) + 1), 1.0, 0.0
    ).astype(BF16)
    lane = lax.broadcasted_iota(jnp.int32, (64, 128), 1)

    w_in.wait()
    for b in range(3):
        flat = jnp.concatenate([w_v[(a * 3 + b) * 3 + c] for a in range(3) for c in range(3)], axis=0)
        high, low = high_low(flat.T)
        if b == 1:
            wf_e[0:128], wf_e[128:256] = high, low
        else:
            at_row = 0 if b == 2 else 128
            wf_o[at_row : at_row + 128] = high
            wf_o[256 + at_row : 384 + at_row] = low

    def split_slab(x):
        high, low = high_low(fine_v[x].reshape(CI * 16, 256))
        for part, dst in ((high, x_hi), (low, x_lo)):
            both = dot(part, split)
            even_t[...] = both[:, :128]
            odd_t[...] = both[:, 128:]
            for y in range(16):
                half, lanes = y % 2, slice(y // 2 * 128, y // 2 * 128 + 128)
                even = even_t[pl.ds(y, CI, stride=16), :]
                odd = odd_t[pl.ds(y, CI, stride=16), :]
                before = jnp.where(lane == 0, 0.0, pltpu.roll(odd, 1, 1))
                for c, value in enumerate((before, even, odd)):
                    rows = slice(x * 192 + c * 64, x * 192 + c * 64 + 64)
                    dst[half, rows, lanes] = value.astype(BF16)

    def operands(mx):
        x0, x1 = ((0, 2), (1, 4), (3, 4))[mx]
        a0 = (1, 0, 0)[mx]
        depth = (x1 - x0) * 192
        return slice(x0 * 192, x1 * 192), slice(a0 * 192, a0 * 192 + depth)

    def forward_rim(mx):
        rows, cols = operands(mx)
        value = dot(wf_o[:, cols], x_hi[1, rows, 896:1024])
        return value[128:256] + value[384:512] + dot(wf_o[128:256, cols], x_lo[1, rows, 896:1024])

    def forward(mx):
        rows, cols = operands(mx)
        target = conv.at[mx]
        target[:, 0:128] = jnp.zeros((CO, 128), F32)

        def chunk(n, carry):
            here = pl.ds(pl.multiple_of(n * 256, 256), 256)
            e_hi, e_lo = x_hi[0, rows, here], x_lo[0, rows, here]
            o_hi, o_lo = x_hi[1, rows, here], x_lo[1, rows, here]
            e = dot(wf_e[:, cols], e_hi)
            e = e[:128] + e[128:] + dot(wf_e[0:128, cols], e_lo)
            o = dot(wf_o[:, cols], o_hi)
            o = o[:256] + o[256:] + dot(wf_o[0:256, cols], o_lo)
            e = e + o[:128]
            target[:, pl.ds(pl.multiple_of(n * 256, 256), 128)] += e[:, :128]
            target[:, pl.ds(pl.multiple_of(n * 256 + 128, 128), 128)] = e[:, 128:] + o[128:, :128]

            target[:, pl.ds(pl.multiple_of(n * 256 + 256, 256), 128)] = o[128:, 128:]
            return carry

        lax.fori_loop(0, 4, chunk, 0)

    out_rows = cells_out.reshape(CO * 32, 128)

    def lanes_of(my):
        return slice(my * 128, my * 128 + 128)

    def store_rows(mx):
        for my in range(8):
            out_rows[pl.ds(FIRST[mx] + my, 128, stride=32), :] = conv[mx, :, lanes_of(my)]
        out_rows[pl.ds(24 + mx, 128, stride=32), :] = conv[mx, :, lanes_of(8)]

    def send_cells(part):
        start, rows = PARTS[part]

        def send(k, carry):
            to = lax.rem(me + k, N_DEV)
            src, dst = (ref.at[i, pl.ds(start, rows)] for ref, i in ((cells_out, to), (cells_in, me)))
            remote(src, dst, conv_send.at[part], conv_recv.at[part], at(to)).start()
            return carry

        lax.fori_loop(1, N_DEV, send, 0)

    fine_in[0].wait()
    split_slab(3)
    forward(2)
    store_rows(2)
    pl.semaphore_wait(barrier, N_DEV - 1)
    to_pair = remote(conv.at[2, :, pl.ds(0, 1024)], pair_x, pair_send.at[4], pair_recv.at[4], pair_device)

    @pl.when(core == 0)
    def _():
        to_pair.start()

    @pl.when(core == 1)
    def _():
        send_cells(0)

    for i, x in ((1, 2), (2, 1)):
        fine_in[i].wait()
        split_slab(x)
    forward(1)
    store_rows(1)
    send_cells(1)
    fine_in[3].wait()
    split_slab(0)
    forward(0)

    @pl.when(core == 0)
    def _():
        to_pair.wait_send()

    @pl.when(core == 1)
    def _():
        to_pair.wait_recv()
        conv[0, :, 0:1024] += pair_x[...]

    store_rows(0)
    send_cells(2)
    cells_in[pl.ds(me, 1)] = cells_out[pl.ds(me, 1)]

    for tap in range(9):
        turned = [w_v[tap * 3 + c] for c in range(3)]
        for half, (now, later) in enumerate(((turned[1], None), (turned[2], turned[0]))):
            rows = slice(tap * 128 + half * 64, tap * 128 + half * 64 + 64)
            for k, block in enumerate((now, later)):
                if block is None:
                    high = low = jnp.zeros((64, 128), BF16)
                else:
                    high, low = high_low(block)
                wb[rows, k * 128 : k * 128 + 128] = high
                wb[rows, 256 + k * 128 : 384 + k * 128] = high
                wb[rows, 512 + k * 128 : 640 + k * 128] = low

    cot_in.wait()
    for part, (start, rows) in enumerate(PARTS):
        if part > 0:
            moved = cells_out.at[pl.ds(0, N_DEV - 1), pl.ds(0, rows)]
            remote(moved, moved, conv_send.at[part], conv_recv.at[part], right).wait()
        else:
            for which in range(2):

                @pl.when(core == which)
                def _(which=which):
                    arrived = cells_in.at[pl.ds(0, N_CHIP - which), pl.ds(0, 8)]
                    remote(arrived, arrived, conv_send.at[0], conv_recv.at[0], right).wait_recv()
                    if which == 1:
                        sent = cells_out.at[pl.ds(0, N_DEV - 1), pl.ds(0, 8)]
                        remote(sent, sent, conv_send.at[0], conv_recv.at[0], right).wait_send()

    first = lax.broadcasted_iota(jnp.int32, (8, 128), 0) == 0

    def device(x, y):
        return x * GY + y

    total = jnp.zeros((8, 128), F32)
    for x in range(GX):
        for y in range(GY):
            for half in range(2):
                tile = cells_in[device(x, y), FIRST[half] : FIRST[half] + 8]
                if y > 0:
                    edge = cells_in[device(x, y - 1), 24 + half : 25 + half]
                    if half == 0 and x > 0:
                        edge += cells_in[device(x - 1, y - 1), 26:27]
                    tile += jnp.where(first, edge, 0.0)
                if half == 0 and x % 2 == 0 and x > 0:
                    tile += cells_in[device(x - 1, y), 0:8]
                whole[2 * x + half, 8 * y : 8 * y + 8] = tile
                total += tile

    def everything_in(value):
        return jnp.sum(jnp.sum(value, axis=1, keepdims=True), axis=0, keepdims=True)

    average = everything_in(total) * (1.0 / CELLS)

    def moment(i, carry):
        away = whole[i] - average
        return carry + jnp.sum((away * away).reshape(8, 8, 128), axis=0)

    spread = everything_in(lax.fori_loop(0, 32, moment, jnp.zeros((8, 128), F32), unroll=4)) * (1.0 / CELLS)
    inv_std = 1.0 / jnp.sqrt(spread + EPSILON)
    own_gain, own_shift = gain[0], shift[0]

    def activate(i, carry):
        s0, s1 = carry
        normed = (whole[i] - average) * inv_std
        pre = own_gain * normed + own_shift
        sig = 1.0 / (1.0 + jnp.exp(-pre))
        act_v[i] = pre * sig
        grad = cot_v[i] * sig * (1.0 + pre * (1.0 - sig))
        cot_v[i] = grad
        whole[i] = normed
        return s0 + jnp.sum(grad.reshape(8, 8, 128), axis=0), s1 + jnp.sum((grad * normed).reshape(8, 8, 128), axis=0)

    sums = lax.fori_loop(0, 32, activate, (jnp.zeros((8, 128), F32), jnp.zeros((8, 128), F32)), unroll=2)
    sum_g, sum_gn = everything_in(sums[0]), everything_in(sums[1])
    gs_out[...] = sum_g * RESCALE
    gg_out[...] = sum_gn * RESCALE
    mean_g, mean_gn = own_gain * sum_g * (1.0 / CELLS), own_gain * sum_gn * (1.0 / CELLS)

    def finish(i, carry):
        whole[i] = inv_std * (own_gain * cot_v[i] - mean_g - whole[i] * mean_gn)
        return carry

    lax.fori_loop(0, 32, finish, 0, unroll=4)
    act_copy = pltpu.make_async_copy(act_v, act_out, local_sem.at[7])
    act_copy.start()
    for x in range(GX):
        for y in range(GY):
            to = device(x, y)
            tiles = pl.ds(8 * y, 8)
            for half in range(2):
                grad_out[to, FIRST[half] : FIRST[half] + 8] = whole[2 * x + half, tiles]
            if x % 2 == 1:
                grad_out[to, 0:8] = whole[2 * x + 2, tiles] if x < GX - 1 else jnp.zeros((8, 128), F32)
            for k in range(3):
                inside = y < GY - 1 and (k < 2 or x < GX - 1)
                grad_out[to, 24 + k : 25 + k] = (
                    whole[2 * x + k, 8 * y + 8 : 8 * y + 9] if inside else jnp.zeros((1, 128), F32)
                )

    grad_in[pl.ds(me, 1)] = grad_out[pl.ds(me, 1)]

    def grad_copy(part, to):
        start, rows = PARTS[part]
        src, dst = (ref.at[i, pl.ds(start, rows)] for ref, i in ((grad_out, to), (grad_in, me)))
        return remote(src, dst, grad_send.at[part], grad_recv.at[part], at(to))

    for part in (2, 1):

        def send(k, carry, part=part):
            grad_copy(part, lax.rem(me + k, N_DEV)).start()
            return carry

        lax.fori_loop(1, N_DEV, send, 0)

    def send_next(k, carry):
        other = lax.rem(chip + k, N_CHIP)
        grad_copy(0, (2 * (other // GY) + 1) * GY + lax.rem(other, GY)).start()
        return carry

    @pl.when(core == 0)
    def _():
        send_next(0, 0)

    lax.fori_loop(1, N_CHIP, send_next, 0)

    def grad_wait(part):
        arrived = grad_in.at[pl.ds(0, N_DEV - 1), pl.ds(0, PARTS[part][1])]
        remote(arrived, arrived, grad_send.at[part], grad_recv.at[part], right).wait_recv()

    wide = lax.broadcasted_iota(jnp.int32, (128, 128), 1)
    grad_rows = grad_in.reshape(CO * 32, 128)

    def place(row, mx, lanes):
        value = grad_rows[pl.ds(row, 128, stride=32), :]
        high, low = high_low(value)
        g_w[mx, 0:128, lanes] = high
        g_w[mx, 128:256, lanes] = low
        g_i[mx, 0:128, lanes] = high
        g_i[mx, 256:384, lanes] = low
        g_i[mx, 512:640, lanes] = high
        moved = jnp.where(wide == 127, 0.0, pltpu.roll(value, 127, 1))
        high, low = high_low(moved)
        g_i[mx, 128:256, lanes] = high
        g_i[mx, 384:512, lanes] = low
        g_i[mx, 640:768, lanes] = high

    def place_rows(mx):
        for my in range(8):
            place(FIRST[mx] + my, mx, lanes_of(my))

    def weight_terms(mx):
        x_rows, cols = operands(mx)
        for b in range(3):
            half = 0 if b == 1 else 1
            here = g_w[mx, :, slice(128, 1152) if b == 0 else slice(0, 1024)]
            both = dot_nt(x_hi[half, x_rows, :], here)
            value = both[:, :128] + both[:, 128:] + dot_nt(x_lo[half, x_rows, :], here[:128])
            for k in range(value.shape[0] // 192):
                a = cols.start // 192 + k
                into = slice((a + 2) % 3 * 576 + b * 192, (a + 2) % 3 * 576 + b * 192 + 192)
                if mx == 0 or (mx == 1 and a == 0):
                    wg[into] = value[192 * k : 192 * k + 192]
                else:
                    wg[into] += value[192 * k : 192 * k + 192]

    def add_to(x, half, lanes, value, fresh):
        if fresh:
            o_acc[x, half, :, lanes] = value
        else:
            o_acc[x, half, :, lanes] += value

    def input_terms(mx):
        taps = [a for a in range(3) if 0 <= 2 * mx - 1 + a <= 3]
        top, bottom = taps[0] * 384, taps[-1] * 384 + 384

        def chunk(n, carry):
            here = pl.ds(pl.multiple_of(n * 256, 256), 256)
            first = pl.ds(pl.multiple_of(n * 256, 256), 128)
            second = pl.ds(pl.multiple_of(n * 256 + 128, 128), 128)
            terms = dot(wb[top:bottom, :], g_i[mx, :, here])
            for a in taps:
                x = 2 * mx - 1 + a
                block = terms[a * 384 - top : a * 384 - top + 384]
                add_to(x, 0, here, block[128:256], a > 0)
                add_to(x, 1, first, block[256:384, :128] + block[0:128, 128:], a > 0)
                add_to(x, 1, second, block[256:384, 128:], a > 0)

                @pl.when(n > 0)
                def _(x=x, block=block):
                    before = pl.ds(pl.multiple_of(n * 256 - 128, 128), 128)
                    o_acc[x, 1, :, before] += block[0:128, :128]

            return carry

        lax.fori_loop(0, 4, chunk, 0)

    def input_terms_rim(mx):
        for a in range(3):
            x = 2 * mx - 1 + a
            if 0 <= x <= 3:
                value = dot(wb[a * 384 : a * 384 + 128, :], g_i[mx, :, 1024:1152])
                o_acc[x, 1, :, 896:1024] += value

    def merge(x):
        slot = x % 2
        if x >= 2:
            for copy in copies[2 * (x - 2) : 2 * (x - 2) + 2]:
                copy.wait()
        for half in range(2):
            blocks = [
                jnp.concatenate([o_acc[x, half, 0:64, lanes_of(my)], o_acc[x, half, 64:128, lanes_of(my)]], axis=1)
                for my in range(8)
            ]
            high, low = high_low(jnp.concatenate(blocks, axis=0))
            merged = dot(high, merge_z) + dot(low, merge_z)
            for my in range(8):
                for z in range(2):
                    out_v[slot, z, pl.ds(2 * my + half, 64, stride=16), :] = merged[
                        64 * my : 64 * my + 64, 128 * z : 128 * z + 128
                    ]
        for z in range(2):
            copy = pltpu.make_async_copy(
                out_v.at[slot, z].reshape(CI, 16, 128),
                gin_out.at[:, x, :, pl.ds(128 * z, 128)],
                out_sem.at[slot, z],
            )
            copy.start()
            copies.append(copy)

    def start_pair(group):
        first, size = GROUPS[group]
        there = wg.at[pl.ds(pl.multiple_of(first + (1 - core) * size, 16), size)]
        copy = remote(there, wg_pair.at[pl.ds(first // 2, size)], pair_send.at[group], pair_recv.at[group], pair_device)
        copy.start()
        return copy

    def chip_device(index):
        return (2 * (index // GY) + core, lax.rem(index, GY))

    def slice_of(index):
        return pl.ds(pl.multiple_of(index * 16, 16), 16)

    def share_out(group, copy):
        first, size = GROUPS[group]
        copy.wait()
        here = wg[pl.ds(pl.multiple_of(first + core * size, 16), size)]
        half = slice(first // 2, first // 2 + size)
        wg_half[half] = here + wg_pair[half]
        owners = (first // 32, (first // 2 + size) // 16)

        def send(k, carry):
            to = lax.rem(chip + k, N_CHIP)

            @pl.when((to >= owners[0]) & (to < owners[1]))
            def _():
                remote(wg_half.at[slice_of(to)], wg_in.at[chip], wr_send, wr_recv, chip_device(to)).start()

            return carry

        lax.fori_loop(1, N_CHIP, send, 0)

    copies = []
    grad_wait(2)
    from_pair = remote(grad_in.at[:, pl.ds(16, 8)], grad_in.at[:, pl.ds(0, 8)], pair_send.at[5], pair_recv.at[5], pair_device)

    @pl.when(core == 1)
    def _():
        from_pair.start()

    place_rows(0)
    for mx in range(3):
        place(24 + mx, mx, lanes_of(8))
    weight_terms(0)
    input_terms(0)
    input_terms_rim(0)
    grad_wait(1)
    place_rows(1)
    weight_terms(1)
    pair_0 = start_pair(0)
    @pl.when(core == 0)
    def _():
        from_pair.wait_recv()

    @pl.when(core == 1)
    def _():
        grad_wait(0)

    place_rows(2)
    weight_terms(2)
    pair_1 = start_pair(1)
    share_out(0, pair_0)
    share_out(1, pair_1)
    input_terms(1)
    input_terms_rim(1)
    input_terms(2)
    input_terms_rim(2)
    own_slice = pl.ds(pl.multiple_of(chip * 16 + jnp.where(chip < CUT, core * 576, 576 + core * 288), 16), 16)

    @pl.when(chip < OWNERS)
    def _():
        wg_in[pl.ds(chip, 1)] = wg_half[slice_of(chip)][None]
        everyone = wg_in.at[pl.ds(0, N_CHIP - 1)]
        remote(everyone, everyone, wr_send, wr_recv, right).wait_recv()
        wg_all[own_slice] = jnp.sum(wg_in[...], axis=0) * RESCALE

    for group in range(2):

        @pl.when((chip < CUT) if group == 0 else (chip >= CUT) & (chip < OWNERS))
        def _(group=group):
            def send_slice(k, carry):
                src = wg_all.at[own_slice]
                to = chip_device(lax.rem(chip + k, N_CHIP))
                remote(src, src, wa_send, wa_recv.at[group], to).start()
                return carry

            lax.fori_loop(1, N_CHIP, send_slice, 0)

    for x in range(4):
        merge(x)
    @pl.when(chip < OWNERS)
    def _():
        some = wg_half.at[pl.ds(0, 16 * (OWNERS - 1))]
        remote(some, some, wr_send, wr_recv, right).wait_send()
        everyone = wg_in.at[pl.ds(0, N_CHIP - 1)]
        remote(everyone, everyone, wa_send, wa_recv.at[0], right).wait_send()

    @pl.when(chip >= OWNERS)
    def _():
        remote(wg_half, wg_half, wr_send, wr_recv, right).wait_send()

    last = []
    for group, (low, high) in enumerate(((0, CUT), (CUT, OWNERS))):
        inside = (chip >= low) & (chip < high)
        for missing in range(2):

            @pl.when(inside if missing else jnp.logical_not(inside))
            def _(group=group, rows=(high - low - missing) * 16):
                some = wg_all.at[pl.ds(0, rows)]
                remote(some, some, wa_send, wa_recv.at[group], right).wait_recv()

        first, size = GROUPS[group]
        done = wg_all.at[pl.ds(pl.multiple_of(first + core * size, 16), size)]
        last.append(remote(done, done, pair_send.at[2 + group], pair_recv.at[2 + group], pair_device))
        last[-1].start()
    for copy in last:
        copy.wait()
    for a in range(3):
        for b in range(3):
            rows = slice((a + 2) % 3 * 576 + b * 192, (a + 2) % 3 * 576 + b * 192 + 192)
            gw_out[(a * 3 + b) * 3 : (a * 3 + b) * 3 + 3] = wg_all[rows].reshape(3, CI, CO)
    for part in (2, 1):
        sent = grad_out.at[pl.ds(0, N_DEV - 1), pl.ds(0, PARTS[part][1])]
        remote(sent, sent, grad_send.at[part], grad_recv.at[part], right).wait_send()
    for which in range(2):

        @pl.when(core == which)
        def _(which=which):
            sent = grad_out.at[pl.ds(0, N_CHIP - which), pl.ds(0, 8)]
            remote(sent, sent, grad_send.at[0], grad_recv.at[0], right).wait_send()
            if which == 1:
                from_pair.wait_send()

    act_copy.wait()
    for copy in copies[4:]:
        copy.wait()


def hand_over(*refs):
    sources, targets, buffers, sem = refs[:3], refs[3:6], refs[6:9], refs[9]
    reads, writes = [], []
    for source, target, buffer, pieces in zip(sources, targets, buffers, (2, 8, 1)):
        size = source.shape[0] // pieces
        for piece in range(pieces):
            here = pl.ds(piece * size, size)
            k = len(reads)
            reads.append(pltpu.make_async_copy(source.at[here], buffer.at[here], sem.at[0, k]))
            writes.append(pltpu.make_async_copy(buffer.at[here], target.at[here], sem.at[1, k]))
    for read in reads:
        read.start()
    for read, write in zip(reads, writes):
        read.wait()
        write.start()
    for write in writes:
        write.wait()


def local(fine_input, weights, norm_gain, norm_shift, cotangent):
    any_space = pl.BlockSpec(memory_space=pl.ANY)
    vmem = pl.BlockSpec(memory_space=pltpu.VMEM)
    smem = pl.BlockSpec(memory_space=pltpu.SMEM)
    dma = pltpu.SemaphoreType.DMA
    activated, grad_input, grad_weights, grad_gain, grad_shift = pl.pallas_call(
        kernel,
        out_shape=(
            jax.ShapeDtypeStruct((32, 64, 128), F32),
            jax.ShapeDtypeStruct((CI, 4, 16, 256), F32),
            jax.ShapeDtypeStruct((27, CI, CO), F32),
            jax.ShapeDtypeStruct((1, 1), F32),
            jax.ShapeDtypeStruct((1, 1), F32),
        ),
        in_specs=[any_space, any_space, smem, smem, any_space],
        out_specs=(any_space, any_space, vmem, vmem, vmem),
        scratch_shapes=[
            pltpu.VMEM((4, CI, 16, 256), F32),
            pltpu.VMEM((27, CI, CO), F32),
            pltpu.VMEM((32, 64, 128), F32),
            pltpu.VMEM((2, 768, 1024), BF16),
            pltpu.VMEM((2, 768, 1024), BF16),
            pltpu.VMEM((1024, 128), F32),
            pltpu.VMEM((1024, 128), F32),
            pltpu.VMEM((256, 576), BF16),
            pltpu.VMEM((512, 576), BF16),
            pltpu.VMEM((1152, 768), BF16),
            pltpu.VMEM((3, CO, 1152), F32),
            pltpu.VMEM((CO, 1024), F32),
            pltpu.VMEM((N_DEV, 32, 128), F32),
            pltpu.VMEM((N_DEV, 32, 128), F32),
            pltpu.VMEM((32, 64, 128), F32),
            pltpu.VMEM((N_DEV, 32, 128), F32),
            pltpu.VMEM((N_DEV, 32, 128), F32),
            pltpu.VMEM((3, 256, 1152), BF16),
            pltpu.VMEM((3, 768, 1152), BF16),
            pltpu.VMEM((4, 2, 128, 1024), F32),
            pltpu.VMEM((2, 2, 1024, 128), F32),
            pltpu.VMEM((32, 64, 128), F32),
            pltpu.VMEM((27 * CI, 128), F32),
            pltpu.VMEM((HALF, 128), F32),
            pltpu.VMEM((HALF, 128), F32),
            pltpu.VMEM((N_CHIP, 16, 128), F32),
            pltpu.VMEM((27 * CI, 128), F32),
            dma((8,)),
            dma((2, 2)),
            dma((3,)),
            dma((3,)),
            dma((3,)),
            dma((3,)),
            dma,
            dma,
            dma,
            dma((2,)),
            dma((6,)),
            dma((6,)),
        ],
        compiler_params=pltpu.CompilerParams(
            collective_id=0, has_side_effects=True, vmem_limit_bytes=60 << 20
        ),
    )(fine_input, weights.transpose(0, 2, 1), norm_gain, norm_shift, cotangent)
    activated, grad_input, grad_weights = pl.pallas_call(
        hand_over,
        out_shape=(
            jax.ShapeDtypeStruct((32, 64, 128), F32),
            jax.ShapeDtypeStruct((CI, 4, 16, 256), F32),
            jax.ShapeDtypeStruct((27, CI, CO), F32),
        ),
        in_specs=[any_space] * 3,
        out_specs=(any_space,) * 3,
        scratch_shapes=[
            pltpu.VMEM((32, 64, 128), F32),
            pltpu.VMEM((CI, 4, 16, 256), F32),
            pltpu.VMEM((27, CI, CO), F32),
            dma((2, 11)),
        ],
        compiler_params=pltpu.CompilerParams(vmem_limit_bytes=60 << 20),
    )(activated, grad_input, grad_weights)
    activated, grad_weights = activated[None], grad_weights.transpose(0, 2, 1)
    return activated, grad_input, grad_weights, grad_gain.reshape(1), grad_shift.reshape(1)


def solution(mesh):
    placed = (
        P(None, "gx", "gy", None),
        P(),
        P(("gx", "gy")),
        P(("gx", "gy")),
        P(("gx", "gy"), None, None, None),
    )
    return jax.shard_map(
        local,
        mesh=mesh,
        in_specs=placed,
        out_specs=(
            P(("gx", "gy"), None, None, None),
            P(None, "gx", "gy", None),
            P(),
            P(("gx", "gy")),
            P(("gx", "gy")),
        ),
        check_vma=False,
    )
```

time: 108 us -> 97.2 us (0.900)
  Pallas kernels: 103 us -> 91.6 us
    pallas_call x1, Pallas kernels: 97 us -> 86.1 us  [local(): pl.pallas_call(kernel, out_shape=(jax.ShapeDtypeStruct((32, 64, 128), F32...]
where the time goes in v3:
time: 97.2 us; the launch traced here: 97 us
  Pallas kernels  91.6 us (94%)
  between operations  5.37 us (6%)
    pallas_call x1, Pallas kernels, local(): pl.pallas_call(kernel, out_shape=(jax.ShapeDtypeStruct((32, 64, 128), F32...  86.1 us
    pallas_call x1, Pallas kernels, local(): pl.pallas_call(hand_over, out_shape=(jax.ShapeDtypeStruct((32, 64, 128),...  5.54 us

profile of v3, /device:TPU:1, one launch (start us, length us, event | category | flops | bytes accessed | tf_op | source)
XLA Modules:
  0.0 97.0 jit_solution(1616025531891641344)
XLA Ops:
  1.9 86.1 %shard_map.92 = (f32[32,64,128]{2,1,0:T(8,128)}, f32[64,4,16,256]{3,2,1,0:T(8,128)}, f32[27,64,128]{2,1,0:T(8,128)}, f32[1,1]{1,0:T(1,128)}, f32[1,1]{1,0:T(1,128)}) custom-call(f32[64,4,16,256]{3,2,1,0:T(8,128)} %fine.1, f32[27,64,128]{2,1,0:T(8,128)} %bitcast.5, f32[1]{0:T(128)S(6)} %copy.12.gain, f32[1]{0:T(128)S(6)} %copy.13.shift, f32[1,32,64,128]{3,2,1,0:T(8,128)} %cot.1), custom_call_target="tpu_custom_call" | custom-call | tf_op jit(solution)/shard_map/pallas_call | solution.py:608
  88.0 5.5 %shard_map.93 = (f32[32,64,128]{2,1,0:T(8,128)}, f32[64,4,16,256]{3,2,1,0:T(8,128)}, f32[27,64,128]{2,1,0:T(8,128)}) custom-call(f32[32,64,128]{2,1,0:T(8,128)} %get-tuple-element.13.refs_0_, f32[64,4,16,256]{3,2,1,0:T(8,128)} %get-tuple-element.14.refs_1_, f32[27,64,128]{2,1,0:T(8,128)} %get-tuple-element.15.refs_2_), custom_call_target="tpu_custom_call" | custom-call | tf_op jit(solution)/shard_map/pallas_call | solution.py:664

commit v4 on v3

--- a/solution.py
+++ b/solution.py
@@ -38,17 +38,13 @@
     return high, (value - high.astype(F32)).astype(BF16)
 
 
-def rows_to_columns(rows):
-    return jnp.concatenate([rows, jnp.zeros((120, 128), F32)], axis=0).T
-
-
 def kernel(
     fine, wts, gain, shift, cot, act_out, gin_out, gw_out, gg_out, gs_out,
     fine_v, w_v, cot_v, x_hi, x_lo, even_t, odd_t, wf_e, wf_o, wb,
-    conv, pair_x, cells_out, cells_in, whole, grad_out, grad_in, g_w, g_i, o_acc, out_v, act_v,
+    conv, pair_x, cells_out, cells_in, whole, grad_out, grad_in, g_w, g_i, o_acc, out_v,
     wg, wg_pair, wg_half, wg_in, wg_all,
     local_sem, out_sem, conv_send, conv_recv, grad_send, grad_recv, wr_send, wr_recv, wa_send, wa_recv,
-    pair_send, pair_recv,
+    pair_send, pair_recv, row_sem,
 ):
     gx, gy = lax.axis_index("gx"), lax.axis_index("gy")
     me = gx * GY + gy
@@ -68,22 +64,23 @@
     fine_in = [
         pltpu.make_async_copy(fine.at[:, x], fine_v.at[x], local_sem.at[x]) for x in (3, 2, 1, 0)
     ]
-    for copy in fine_in:
+    w_in = pltpu.make_async_copy(wts, w_v, local_sem.at[4])
+    cot_in = pltpu.make_async_copy(cot.at[0], cot_v, local_sem.at[5])
+    for copy in (w_in, *fine_in, cot_in):
         copy.start()
-    w_in = pltpu.make_async_copy(wts, w_v, local_sem.at[4])
-    w_in.start()
-    cot_in = pltpu.make_async_copy(cot.at[0], cot_v, local_sem.at[5])
-    cot_in.start()
 
     barrier = pltpu.get_barrier_semaphore()
 
-    def greet(k, carry):
-        pl.semaphore_signal(
-            barrier, inc=1, device_id=at(lax.rem(me + k, N_DEV)), device_id_type=MESH
-        )
-        return carry
-
-    lax.fori_loop(1, N_DEV, greet, 0)
+    def greet(sem, sizes):
+        for count, device in zip(sizes, (lambda k: (lax.rem(gx + k, GX), gy), lambda k: (gx, lax.rem(gy + k, GY)))):
+
+            def one(k, carry, device=device):
+                pl.semaphore_signal(sem, inc=1, device_id=device(k), device_id_type=MESH)
+                return carry
+
+            lax.fori_loop(1, count, one, 0)
+
+    greet(barrier, (GX, GY))
 
     row = lax.broadcasted_iota(jnp.int32, (256, 256), 0)
     col = lax.broadcasted_iota(jnp.int32, (256, 256), 1)
@@ -173,13 +170,15 @@
             remote(src, dst, conv_send.at[part], conv_recv.at[part], at(to)).start()
             return carry
 
-        lax.fori_loop(1, N_DEV, send, 0)
+        lax.fori_loop(2, N_DEV, send, send(1, 0), unroll=6)
 
     fine_in[0].wait()
     split_slab(3)
+    pl.semaphore_wait(barrier, GX + GY - 2)
+    greet(row_sem, (GX,))
     forward(2)
     store_rows(2)
-    pl.semaphore_wait(barrier, N_DEV - 1)
+    pl.semaphore_wait(row_sem, GX - 1)
     to_pair = remote(conv.at[2, :, pl.ds(0, 1024)], pair_x, pair_send.at[4], pair_recv.at[4], pair_device)
 
     @pl.when(core == 0)
@@ -280,7 +279,7 @@
         normed = (whole[i] - average) * inv_std
         pre = own_gain * normed + own_shift
         sig = 1.0 / (1.0 + jnp.exp(-pre))
-        act_v[i] = pre * sig
+        act_out[i] = pre * sig
         grad = cot_v[i] * sig * (1.0 + pre * (1.0 - sig))
         cot_v[i] = grad
         whole[i] = normed
@@ -297,8 +296,6 @@
         return carry
 
     lax.fori_loop(0, 32, finish, 0, unroll=4)
-    act_copy = pltpu.make_async_copy(act_v, act_out, local_sem.at[7])
-    act_copy.start()
     for x in range(GX):
         for y in range(GY):
             to = device(x, y)
@@ -326,7 +323,7 @@
             grad_copy(part, lax.rem(me + k, N_DEV)).start()
             return carry
 
-        lax.fori_loop(1, N_DEV, send, 0)
+        lax.fori_loop(2, N_DEV, send, send(1, 0), unroll=6)
 
     def send_next(k, carry):
         other = lax.rem(chip + k, N_CHIP)
@@ -576,28 +573,8 @@
             if which == 1:
                 from_pair.wait_send()
 
-    act_copy.wait()
     for copy in copies[4:]:
         copy.wait()
-
-
-def hand_over(*refs):
-    sources, targets, buffers, sem = refs[:3], refs[3:6], refs[6:9], refs[9]
-    reads, writes = [], []
-    for source, target, buffer, pieces in zip(sources, targets, buffers, (2, 8, 1)):
-        size = source.shape[0] // pieces
-        for piece in range(pieces):
-            here = pl.ds(piece * size, size)
-            k = len(reads)
-            reads.append(pltpu.make_async_copy(source.at[here], buffer.at[here], sem.at[0, k]))
-            writes.append(pltpu.make_async_copy(buffer.at[here], target.at[here], sem.at[1, k]))
-    for read in reads:
-        read.start()
-    for read, write in zip(reads, writes):
-        read.wait()
-        write.start()
-    for write in writes:
-        write.wait()
 
 
 def local(fine_input, weights, norm_gain, norm_shift, cotangent):
@@ -608,14 +585,14 @@
     activated, grad_input, grad_weights, grad_gain, grad_shift = pl.pallas_call(
         kernel,
         out_shape=(
-            jax.ShapeDtypeStruct((32, 64, 128), F32),
-            jax.ShapeDtypeStruct((CI, 4, 16, 256), F32),
-            jax.ShapeDtypeStruct((27, CI, CO), F32),
+            pltpu.VMEM((32, 64, 128), F32),
+            pltpu.VMEM((CI, 4, 16, 256), F32),
+            pltpu.VMEM((27, CI, CO), F32),
             jax.ShapeDtypeStruct((1, 1), F32),
             jax.ShapeDtypeStruct((1, 1), F32),
         ),
         in_specs=[any_space, any_space, smem, smem, any_space],
-        out_specs=(any_space, any_space, vmem, vmem, vmem),
+        out_specs=(vmem,) * 5,
         scratch_shapes=[
             pltpu.VMEM((4, CI, 16, 256), F32),
             pltpu.VMEM((27, CI, CO), F32),
@@ -638,7 +615,6 @@
             pltpu.VMEM((3, 768, 1152), BF16),
             pltpu.VMEM((4, 2, 128, 1024), F32),
             pltpu.VMEM((2, 2, 1024, 128), F32),
-            pltpu.VMEM((32, 64, 128), F32),
             pltpu.VMEM((27 * CI, 128), F32),
             pltpu.VMEM((HALF, 128), F32),
             pltpu.VMEM((HALF, 128), F32),
@@ -656,28 +632,12 @@
             dma((2,)),
             dma((6,)),
             dma((6,)),
+            pltpu.SemaphoreType.REGULAR,
         ],
         compiler_params=pltpu.CompilerParams(
-            collective_id=0, has_side_effects=True, vmem_limit_bytes=60 << 20
+            collective_id=0, has_side_effects=True, vmem_limit_bytes=50 << 20
         ),
     )(fine_input, weights.transpose(0, 2, 1), norm_gain, norm_shift, cotangent)
-    activated, grad_input, grad_weights = pl.pallas_call(
-        hand_over,
-        out_shape=(
-            jax.ShapeDtypeStruct((32, 64, 128), F32),
-            jax.ShapeDtypeStruct((CI, 4, 16, 256), F32),
-            jax.ShapeDtypeStruct((27, CI, CO), F32),
-        ),
-        in_specs=[any_space] * 3,
-        out_specs=(any_space,) * 3,
-        scratch_shapes=[
-            pltpu.VMEM((32, 64, 128), F32),
-            pltpu.VMEM((CI, 4, 16, 256), F32),
-            pltpu.VMEM((27, CI, CO), F32),
-            dma((2, 11)),
-        ],
-        compiler_params=pltpu.CompilerParams(vmem_limit_bytes=60 << 20),
-    )(activated, grad_input, grad_weights)
     activated, grad_weights = activated[None], grad_weights.transpose(0, 2, 1)
     return activated, grad_input, grad_weights, grad_gain.reshape(1), grad_shift.reshape(1)
 

time: 97.2 us -> 93.4 us (0.961)
  Pallas kernels: 91.6 us -> 84 us
  local copies, waits for them, and re-layouts: 0 us -> 3.9 us
    pallas_call x2 -> x1, Pallas kernels: 91.6 us -> 84 us  [local(): pl.pallas_call(kernel, out_shape=(pltpu.VMEM((32, 64, 128), F32), pltpu.V...]
    unnamed x0 -> x3, local copies, waits for them, and re-layouts: none -> 3.9 us
where the time goes in v4:
time: 93.4 us; the launch traced here: 93.3 us
  Pallas kernels  84 us (90%)
  between operations  5.38 us (6%)
  local copies, waits for them, and re-layouts  3.9 us (4%)
    pallas_call x1, Pallas kernels, local(): pl.pallas_call(kernel, out_shape=(pltpu.VMEM((32, 64, 128), F32), pltpu.V...  84 us
    unnamed x3, local copies, waits for them, and re-layouts  3.9 us

profile of v4, /device:TPU:1, one launch (start us, length us, event | category | flops | bytes accessed | tf_op | source)
XLA Modules:
  0.0 93.3 jit_solution(7169902238113349167)
XLA Ops:
  1.9 84.0 %shard_map.92 = (f32[32,64,128]{2,1,0:T(8,128)S(1)}, f32[64,4,16,256]{3,2,1,0:T(8,128)S(1)}, f32[27,64,128]{2,1,0:T(8,128)S(1)}, f32[1,1]{1,0:T(1,128)}, f32[1,1]{1,0:T(1,128)}) custom-call(f32[64,4,16,256]{3,2,1,0:T(8,128)} %fine.1, f32[27,64,128]{2,1,0:T(8,128)} %bitcast.7, f32[1]{0:T(128)S(6)} %copy.18.gain, f32[1]{0:T(128)S(6)} %copy.19.shift, ...), custom_call_target="tpu_custom_call" | custom-call | tf_op jit(solution)/shard_map/pallas_call | solution.py:585
  85.9 1.0 %copy.15 = f32[1,32,64,128]{3,2,1,0:T(8,128)} copy(f32[1,32,64,128]{3,2,1,0:T(8,128)S(1)} %bitcast.5) | data formatting | bytes 2097152
  86.9 0.9 copy.17
  87.8 2.0 %copy.16 = f32[64,4,16,256]{3,2,1,0:T(8,128)} copy(f32[64,4,16,256]{3,2,1,0:T(8,128)S(1)} %get-tuple-element.16) | data formatting | bytes 8388608

commit v5 on v4

--- a/solution.py
+++ b/solution.py
@@ -21,7 +21,8 @@
 OWNERS = HALF // 16
 FIRST = (16, 8, 0)
 PARTS = ((0, 8), (8, 8), (16, 11))
-GROUPS = ((0, 576), (1152, 288))
+GROUPS = ((576, 576), (0, 288))
+HALVES = (0, 576)
 CUT = 36
 
 
@@ -42,7 +43,7 @@
     fine, wts, gain, shift, cot, act_out, gin_out, gw_out, gg_out, gs_out,
     fine_v, w_v, cot_v, x_hi, x_lo, even_t, odd_t, wf_e, wf_o, wb,
     conv, pair_x, cells_out, cells_in, whole, grad_out, grad_in, g_w, g_i, o_acc, out_v,
-    wg, wg_pair, wg_half, wg_in, wg_all,
+    wg, wg_pair, wg_half, wg_in,
     local_sem, out_sem, conv_send, conv_recv, grad_send, grad_recv, wr_send, wr_recv, wa_send, wa_recv,
     pair_send, pair_recv, row_sem,
 ):
@@ -334,7 +335,7 @@
     def _():
         send_next(0, 0)
 
-    lax.fori_loop(1, N_CHIP, send_next, 0)
+    lax.fori_loop(1, N_CHIP, send_next, 0, unroll=7)
 
     def grad_wait(part):
         arrived = grad_in.at[pl.ds(0, N_DEV - 1), pl.ds(0, PARTS[part][1])]
@@ -343,23 +344,23 @@
     wide = lax.broadcasted_iota(jnp.int32, (128, 128), 1)
     grad_rows = grad_in.reshape(CO * 32, 128)
 
-    def place(row, mx, lanes):
-        value = grad_rows[pl.ds(row, 128, stride=32), :]
-        high, low = high_low(value)
-        g_w[mx, 0:128, lanes] = high
-        g_w[mx, 128:256, lanes] = low
-        g_i[mx, 0:128, lanes] = high
-        g_i[mx, 256:384, lanes] = low
-        g_i[mx, 512:640, lanes] = high
-        moved = jnp.where(wide == 127, 0.0, pltpu.roll(value, 127, 1))
-        high, low = high_low(moved)
-        g_i[mx, 128:256, lanes] = high
-        g_i[mx, 384:512, lanes] = low
-        g_i[mx, 640:768, lanes] = high
-
-    def place_rows(mx):
-        for my in range(8):
-            place(FIRST[mx] + my, mx, lanes_of(my))
+    def rows_of(mx):
+        yield from ((FIRST[mx] + my, lanes_of(my)) for my in range(8))
+
+    def place_w(mx, rows):
+        for row, lanes in rows:
+            high, low = high_low(grad_rows[pl.ds(row, 128, stride=32), :])
+            g_w[mx, 0:128, lanes] = high
+            g_w[mx, 128:256, lanes] = low
+
+    def place_i(mx, rows):
+        for row, lanes in rows:
+            value = grad_rows[pl.ds(row, 128, stride=32), :]
+            for k, part in enumerate((value, jnp.where(wide == 127, 0.0, pltpu.roll(value, 127, 1)))):
+                high, low = high_low(part)
+                g_i[mx, 128 * k : 128 * k + 128, lanes] = high
+                g_i[mx, 256 + 128 * k : 384 + 128 * k, lanes] = low
+                g_i[mx, 512 + 128 * k : 640 + 128 * k, lanes] = high
 
     def weight_terms(mx):
         x_rows, cols = operands(mx)
@@ -370,7 +371,7 @@
             value = both[:, :128] + both[:, 128:] + dot_nt(x_lo[half, x_rows, :], here[:128])
             for k in range(value.shape[0] // 192):
                 a = cols.start // 192 + k
-                into = slice((a + 2) % 3 * 576 + b * 192, (a + 2) % 3 * 576 + b * 192 + 192)
+                into = slice(a * 576 + b * 192, a * 576 + b * 192 + 192)
                 if mx == 0 or (mx == 1 and a == 0):
                     wg[into] = value[192 * k : 192 * k + 192]
                 else:
@@ -443,7 +444,7 @@
     def start_pair(group):
         first, size = GROUPS[group]
         there = wg.at[pl.ds(pl.multiple_of(first + (1 - core) * size, 16), size)]
-        copy = remote(there, wg_pair.at[pl.ds(first // 2, size)], pair_send.at[group], pair_recv.at[group], pair_device)
+        copy = remote(there, wg_pair.at[pl.ds(HALVES[group], size)], pair_send.at[group], pair_recv.at[group], pair_device)
         copy.start()
         return copy
 
@@ -457,20 +458,20 @@
         first, size = GROUPS[group]
         copy.wait()
         here = wg[pl.ds(pl.multiple_of(first + core * size, 16), size)]
-        half = slice(first // 2, first // 2 + size)
+        half = slice(HALVES[group], HALVES[group] + size)
         wg_half[half] = here + wg_pair[half]
-        owners = (first // 32, (first // 2 + size) // 16)
+        low, count = HALVES[group] // 16, size // 16
 
         def send(k, carry):
-            to = lax.rem(chip + k, N_CHIP)
-
-            @pl.when((to >= owners[0]) & (to < owners[1]))
+            to = low + lax.rem(chip + k, count)
+
+            @pl.when(to != chip)
             def _():
                 remote(wg_half.at[slice_of(to)], wg_in.at[chip], wr_send, wr_recv, chip_device(to)).start()
 
             return carry
 
-        lax.fori_loop(1, N_CHIP, send, 0)
+        lax.fori_loop(0, count, send, 0, unroll=6)
 
     copies = []
     grad_wait(2)
@@ -480,14 +481,18 @@
     def _():
         from_pair.start()
 
-    place_rows(0)
+    by_y = [(24 + mx, lanes_of(8)) for mx in range(3)]
+    place_w(0, rows_of(0))
     for mx in range(3):
-        place(24 + mx, mx, lanes_of(8))
+        place_w(mx, by_y[mx : mx + 1])
     weight_terms(0)
+    for mx in range(3):
+        place_i(mx, by_y[mx : mx + 1])
+    place_i(0, rows_of(0))
     input_terms(0)
     input_terms_rim(0)
     grad_wait(1)
-    place_rows(1)
+    place_w(1, rows_of(1))
     weight_terms(1)
     pair_0 = start_pair(0)
     @pl.when(core == 0)
@@ -498,35 +503,37 @@
     def _():
         grad_wait(0)
 
-    place_rows(2)
+    place_w(2, rows_of(2))
     weight_terms(2)
     pair_1 = start_pair(1)
     share_out(0, pair_0)
     share_out(1, pair_1)
+    place_i(1, rows_of(1))
     input_terms(1)
     input_terms_rim(1)
+    place_i(2, rows_of(2))
     input_terms(2)
     input_terms_rim(2)
-    own_slice = pl.ds(pl.multiple_of(chip * 16 + jnp.where(chip < CUT, core * 576, 576 + core * 288), 16), 16)
+    own_slice = pl.ds(pl.multiple_of(chip * 16 + jnp.where(chip < CUT, 576 + core * 576, core * 288 - 576), 16), 16)
 
     @pl.when(chip < OWNERS)
     def _():
         wg_in[pl.ds(chip, 1)] = wg_half[slice_of(chip)][None]
         everyone = wg_in.at[pl.ds(0, N_CHIP - 1)]
         remote(everyone, everyone, wr_send, wr_recv, right).wait_recv()
-        wg_all[own_slice] = jnp.sum(wg_in[...], axis=0) * RESCALE
+        gw_out[own_slice] = jnp.sum(wg_in[...], axis=0) * RESCALE
 
     for group in range(2):
 
         @pl.when((chip < CUT) if group == 0 else (chip >= CUT) & (chip < OWNERS))
         def _(group=group):
             def send_slice(k, carry):
-                src = wg_all.at[own_slice]
+                src = gw_out.at[own_slice]
                 to = chip_device(lax.rem(chip + k, N_CHIP))
                 remote(src, src, wa_send, wa_recv.at[group], to).start()
                 return carry
 
-            lax.fori_loop(1, N_CHIP, send_slice, 0)
+            lax.fori_loop(1, N_CHIP, send_slice, 0, unroll=7)
 
     for x in range(4):
         merge(x)
@@ -548,19 +555,15 @@
 
             @pl.when(inside if missing else jnp.logical_not(inside))
             def _(group=group, rows=(high - low - missing) * 16):
-                some = wg_all.at[pl.ds(0, rows)]
+                some = gw_out.at[pl.ds(0, rows)]
                 remote(some, some, wa_send, wa_recv.at[group], right).wait_recv()
 
         first, size = GROUPS[group]
-        done = wg_all.at[pl.ds(pl.multiple_of(first + core * size, 16), size)]
+        done = gw_out.at[pl.ds(pl.multiple_of(first + core * size, 16), size)]
         last.append(remote(done, done, pair_send.at[2 + group], pair_recv.at[2 + group], pair_device))
         last[-1].start()
     for copy in last:
         copy.wait()
-    for a in range(3):
-        for b in range(3):
-            rows = slice((a + 2) % 3 * 576 + b * 192, (a + 2) % 3 * 576 + b * 192 + 192)
-            gw_out[(a * 3 + b) * 3 : (a * 3 + b) * 3 + 3] = wg_all[rows].reshape(3, CI, CO)
     for part in (2, 1):
         sent = grad_out.at[pl.ds(0, N_DEV - 1), pl.ds(0, PARTS[part][1])]
         remote(sent, sent, grad_send.at[part], grad_recv.at[part], right).wait_send()
@@ -574,6 +577,19 @@
                 from_pair.wait_send()
 
     for copy in copies[4:]:
+        copy.wait()
+
+
+def hand_over(*refs):
+    copies = []
+    for source, target, pieces in zip(refs[:3], refs[3:6], (2, 8, 1)):
+        size = source.shape[0] // pieces
+        for piece in range(pieces):
+            here = pl.ds(piece * size, size)
+            copies.append(pltpu.make_async_copy(source.at[here], target.at[here], refs[6].at[len(copies)]))
+    for copy in copies:
+        copy.start()
+    for copy in copies:
         copy.wait()
 
 
@@ -587,7 +603,7 @@
         out_shape=(
             pltpu.VMEM((32, 64, 128), F32),
             pltpu.VMEM((CI, 4, 16, 256), F32),
-            pltpu.VMEM((27, CI, CO), F32),
+            pltpu.VMEM((27 * CI, CO), F32),
             jax.ShapeDtypeStruct((1, 1), F32),
             jax.ShapeDtypeStruct((1, 1), F32),
         ),
@@ -619,7 +635,6 @@
             pltpu.VMEM((HALF, 128), F32),
             pltpu.VMEM((HALF, 128), F32),
             pltpu.VMEM((N_CHIP, 16, 128), F32),
-            pltpu.VMEM((27 * CI, 128), F32),
             dma((8,)),
             dma((2, 2)),
             dma((3,)),
@@ -638,7 +653,15 @@
             collective_id=0, has_side_effects=True, vmem_limit_bytes=50 << 20
         ),
     )(fine_input, weights.transpose(0, 2, 1), norm_gain, norm_shift, cotangent)
-    activated, grad_weights = activated[None], grad_weights.transpose(0, 2, 1)
+    activated, grad_input, grad_weights = pl.pallas_call(
+        hand_over,
+        out_shape=tuple(jax.ShapeDtypeStruct(v.shape, F32) for v in (activated, grad_input, grad_weights)),
+        in_specs=[any_space] * 3,
+        out_specs=(any_space,) * 3,
+        scratch_shapes=[dma((11,))],
+        compiler_params=pltpu.CompilerParams(vmem_limit_bytes=1 << 20),
+    )(activated, grad_input, grad_weights)
+    activated, grad_weights = activated[None], grad_weights.reshape(27, CI, CO).transpose(0, 2, 1)
     return activated, grad_input, grad_weights, grad_gain.reshape(1), grad_shift.reshape(1)
 
 

time: 93.4 us -> 92.6 us (level)
  local copies, waits for them, and re-layouts: 3.9 us -> 0 us
  Pallas kernels: 84 us -> 87 us
    unnamed x3 -> x0, local copies, waits for them, and re-layouts: 3.9 us -> none
    pallas_call x0 -> x1, Pallas kernels: none -> 2.71 us  [local(): pl.pallas_call(hand_over, out_shape=tuple((jax.ShapeDtypeStruct(v.shape,...]
where the time goes in v5:
time: 92.6 us; the launch traced here: 92.4 us
  Pallas kernels  87 us (94%)
  between operations  5.46 us (6%)
    pallas_call x1, Pallas kernels, local(): pl.pallas_call(kernel, out_shape=(pltpu.VMEM((32, 64, 128), F32), pltpu.V...  84.3 us
    pallas_call x1, Pallas kernels, local(): pl.pallas_call(hand_over, out_shape=tuple((jax.ShapeDtypeStruct(v.shape,...  2.71 us

profile of v5, /device:TPU:1, one launch (start us, length us, event | category | flops | bytes accessed | tf_op | source)
XLA Modules:
  0.0 92.4 jit_solution(12230477425714396319)
XLA Ops:
  1.9 84.3 %shard_map.92 = (f32[32,64,128]{2,1,0:T(8,128)S(1)}, f32[64,4,16,256]{3,2,1,0:T(8,128)S(1)}, f32[1728,128]{1,0:T(8,128)S(1)}, f32[1,1]{1,0:T(1,128)}, f32[1,1]{1,0:T(1,128)}) custom-call(f32[64,4,16,256]{3,2,1,0:T(8,128)} %fine.1, f32[27,64,128]{2,1,0:T(8,128)} %bitcast.7, f32[1]{0:T(128)S(6)} %copy.12.gain, f32[1]{0:T(128)S(6)} %copy.13.shift, ...), custom_call_target="tpu_custom_call" | custom-call | tf_op jit(solution)/shard_map/pallas_call | solution.py:601
  86.2 2.7 %shard_map.93 = (f32[32,64,128]{2,1,0:T(8,128)}, f32[64,4,16,256]{3,2,1,0:T(8,128)}, f32[1728,128]{1,0:T(8,128)}) custom-call(f32[32,64,128]{2,1,0:T(8,128)S(1)} %get-tuple-element.13.refs_0_, f32[64,4,16,256]{3,2,1,0:T(8,128)S(1)} %get-tuple-element.14.refs_1_, f32[1728,128]{1,0:T(8,128)S(1)} %get-tuple-element.15.refs_2_), custom_call_target="tpu_custom_call" | custom-call | tf_op jit(solution)/shard_map/pallas_call | solution.py:656

commit v6 on v5

--- a/solution.py
+++ b/solution.py
@@ -166,7 +166,7 @@
         start, rows = PARTS[part]
 
         def send(k, carry):
-            to = lax.rem(me + k, N_DEV)
+            to = lax.rem(me + k + core * (N_DEV - 2 * k), N_DEV)
             src, dst = (ref.at[i, pl.ds(start, rows)] for ref, i in ((cells_out, to), (cells_in, me)))
             remote(src, dst, conv_send.at[part], conv_recv.at[part], at(to)).start()
             return carry
@@ -321,13 +321,13 @@
     for part in (2, 1):
 
         def send(k, carry, part=part):
-            grad_copy(part, lax.rem(me + k, N_DEV)).start()
+            grad_copy(part, lax.rem(me + k + core * (N_DEV - 2 * k), N_DEV)).start()
             return carry
 
         lax.fori_loop(2, N_DEV, send, send(1, 0), unroll=6)
 
     def send_next(k, carry):
-        other = lax.rem(chip + k, N_CHIP)
+        other = lax.rem(chip + k + core * (N_CHIP - 2 * k), N_CHIP)
         grad_copy(0, (2 * (other // GY) + 1) * GY + lax.rem(other, GY)).start()
         return carry
 
@@ -463,7 +463,7 @@
         low, count = HALVES[group] // 16, size // 16
 
         def send(k, carry):
-            to = low + lax.rem(chip + k, count)
+            to = low + lax.rem(chip + k + core * (count - 2 * k), count)
 
             @pl.when(to != chip)
             def _():
@@ -529,7 +529,7 @@
         def _(group=group):
             def send_slice(k, carry):
                 src = gw_out.at[own_slice]
-                to = chip_device(lax.rem(chip + k, N_CHIP))
+                to = chip_device(lax.rem(chip + k + core * (N_CHIP - 2 * k), N_CHIP))
                 remote(src, src, wa_send, wa_recv.at[group], to).start()
                 return carry
 

time: 92.6 us -> 91.2 us (0.985)
  Pallas kernels: 87 us -> 85.6 us
    pallas_call x1, Pallas kernels: 84.3 us -> 82.9 us  [local(): pl.pallas_call(kernel, out_shape=(pltpu.VMEM((32, 64, 128), F32), pltpu.V...]
where the time goes in v6:
time: 91.2 us; the launch traced here: 91.1 us
  Pallas kernels  85.6 us (94%)
  between operations  5.46 us (6%)
    pallas_call x1, Pallas kernels, local(): pl.pallas_call(kernel, out_shape=(pltpu.VMEM((32, 64, 128), F32), pltpu.V...  82.9 us
    pallas_call x1, Pallas kernels, local(): pl.pallas_call(hand_over, out_shape=tuple((jax.ShapeDtypeStruct(v.shape,...  2.71 us

profile of v6, /device:TPU:1, one launch (start us, length us, event | category | flops | bytes accessed | tf_op | source)
XLA Modules:
  0.0 91.1 jit_solution(2125138806221208193)
XLA Ops:
  1.9 82.9 %shard_map.92 = (f32[32,64,128]{2,1,0:T(8,128)S(1)}, f32[64,4,16,256]{3,2,1,0:T(8,128)S(1)}, f32[1728,128]{1,0:T(8,128)S(1)}, f32[1,1]{1,0:T(1,128)}, f32[1,1]{1,0:T(1,128)}) custom-call(f32[64,4,16,256]{3,2,1,0:T(8,128)} %fine.1, f32[27,64,128]{2,1,0:T(8,128)} %bitcast.7, f32[1]{0:T(128)S(6)} %copy.12.gain, f32[1]{0:T(128)S(6)} %copy.13.shift, ...), custom_call_target="tpu_custom_call" | custom-call | tf_op jit(solution)/shard_map/pallas_call | solution.py:601
  84.9 2.7 %shard_map.93 = (f32[32,64,128]{2,1,0:T(8,128)}, f32[64,4,16,256]{3,2,1,0:T(8,128)}, f32[1728,128]{1,0:T(8,128)}) custom-call(f32[32,64,128]{2,1,0:T(8,128)S(1)} %get-tuple-element.13.refs_0_, f32[64,4,16,256]{3,2,1,0:T(8,128)S(1)} %get-tuple-element.14.refs_1_, f32[1728,128]{1,0:T(8,128)S(1)} %get-tuple-element.15.refs_2_), custom_call_target="tpu_custom_call" | custom-call | tf_op jit(solution)/shard_map/pallas_call | solution.py:656

commit v7 on v6

--- a/solution.py
+++ b/solution.py
@@ -108,8 +108,8 @@
         high, low = high_low(fine_v[x].reshape(CI * 16, 256))
         for part, dst in ((high, x_hi), (low, x_lo)):
             both = dot(part, split)
-            even_t[...] = both[:, :128]
-            odd_t[...] = both[:, 128:]
+            even_t[0:1024] = both[:, :128]
+            odd_t[0:1024] = both[:, 128:]
             for y in range(16):
                 half, lanes = y % 2, slice(y // 2 * 128, y // 2 * 128 + 128)
                 even = even_t[pl.ds(y, CI, stride=16), :]
@@ -152,7 +152,7 @@
 
         lax.fori_loop(0, 4, chunk, 0)
 
-    out_rows = cells_out.reshape(CO * 32, 128)
+    out_rows = cells_out.reshape((CO + 1) * 32, 128)
 
     def lanes_of(my):
         return slice(my * 128, my * 128 + 128)
@@ -342,7 +342,7 @@
         remote(arrived, arrived, grad_send.at[part], grad_recv.at[part], right).wait_recv()
 
     wide = lax.broadcasted_iota(jnp.int32, (128, 128), 1)
-    grad_rows = grad_in.reshape(CO * 32, 128)
+    grad_rows = grad_in.reshape((CO + 1) * 32, 128)
 
     def rows_of(mx):
         yield from ((FIRST[mx] + my, lanes_of(my)) for my in range(8))
@@ -434,7 +434,7 @@
                     ]
         for z in range(2):
             copy = pltpu.make_async_copy(
-                out_v.at[slot, z].reshape(CI, 16, 128),
+                out_v.at[slot, z, pl.ds(0, 1024)].reshape(CI, 16, 128),
                 gin_out.at[:, x, :, pl.ds(128 * z, 128)],
                 out_sem.at[slot, z],
             )
@@ -475,7 +475,7 @@
 
     copies = []
     grad_wait(2)
-    from_pair = remote(grad_in.at[:, pl.ds(16, 8)], grad_in.at[:, pl.ds(0, 8)], pair_send.at[5], pair_recv.at[5], pair_device)
+    from_pair = remote(grad_in.at[pl.ds(0, CO), pl.ds(16, 8)], grad_in.at[pl.ds(0, CO), pl.ds(0, 8)], pair_send.at[5], pair_recv.at[5], pair_device)
 
     @pl.when(core == 1)
     def _():
@@ -615,22 +615,22 @@
             pltpu.VMEM((32, 64, 128), F32),
             pltpu.VMEM((2, 768, 1024), BF16),
             pltpu.VMEM((2, 768, 1024), BF16),
-            pltpu.VMEM((1024, 128), F32),
-            pltpu.VMEM((1024, 128), F32),
+            pltpu.VMEM((1040, 128), F32),
+            pltpu.VMEM((1040, 128), F32),
             pltpu.VMEM((256, 576), BF16),
             pltpu.VMEM((512, 576), BF16),
             pltpu.VMEM((1152, 768), BF16),
             pltpu.VMEM((3, CO, 1152), F32),
             pltpu.VMEM((CO, 1024), F32),
-            pltpu.VMEM((N_DEV, 32, 128), F32),
+            pltpu.VMEM((N_DEV + 1, 32, 128), F32),
             pltpu.VMEM((N_DEV, 32, 128), F32),
             pltpu.VMEM((32, 64, 128), F32),
             pltpu.VMEM((N_DEV, 32, 128), F32),
-            pltpu.VMEM((N_DEV, 32, 128), F32),
+            pltpu.VMEM((N_DEV + 1, 32, 128), F32),
             pltpu.VMEM((3, 256, 1152), BF16),
             pltpu.VMEM((3, 768, 1152), BF16),
             pltpu.VMEM((4, 2, 128, 1024), F32),
-            pltpu.VMEM((2, 2, 1024, 128), F32),
+            pltpu.VMEM((2, 2, 1040, 128), F32),
             pltpu.VMEM((27 * CI, 128), F32),
             pltpu.VMEM((HALF, 128), F32),
             pltpu.VMEM((HALF, 128), F32),

time: 91.2 us -> 91.2 us (level)
  no operation moved by 1% of the time
where the time goes in v7:
time: 91.2 us; the launch traced here: 91 us
  Pallas kernels  85.6 us (94%)
  between operations  5.46 us (6%)
    pallas_call x1, Pallas kernels, local(): pl.pallas_call(kernel, out_shape=(pltpu.VMEM((32, 64, 128), F32), pltpu.V...  82.9 us
    pallas_call x1, Pallas kernels, local(): pl.pallas_call(hand_over, out_shape=tuple((jax.ShapeDtypeStruct(v.shape,...  2.71 us

profile of v7, /device:TPU:1, one launch (start us, length us, event | category | flops | bytes accessed | tf_op | source)
XLA Modules:
  0.0 91.0 jit_solution(6086174241659062578)
XLA Ops:
  1.9 82.9 %shard_map.92 = (f32[32,64,128]{2,1,0:T(8,128)S(1)}, f32[64,4,16,256]{3,2,1,0:T(8,128)S(1)}, f32[1728,128]{1,0:T(8,128)S(1)}, f32[1,1]{1,0:T(1,128)}, f32[1,1]{1,0:T(1,128)}) custom-call(f32[64,4,16,256]{3,2,1,0:T(8,128)} %fine.1, f32[27,64,128]{2,1,0:T(8,128)} %bitcast.7, f32[1]{0:T(128)S(6)} %copy.12.gain, f32[1]{0:T(128)S(6)} %copy.13.shift, ...), custom_call_target="tpu_custom_call" | custom-call | tf_op jit(solution)/shard_map/pallas_call | solution.py:601
  84.8 2.7 %shard_map.93 = (f32[32,64,128]{2,1,0:T(8,128)}, f32[64,4,16,256]{3,2,1,0:T(8,128)}, f32[1728,128]{1,0:T(8,128)}) custom-call(f32[32,64,128]{2,1,0:T(8,128)S(1)} %get-tuple-element.13.refs_0_, f32[64,4,16,256]{3,2,1,0:T(8,128)S(1)} %get-tuple-element.14.refs_1_, f32[1728,128]{1,0:T(8,128)S(1)} %get-tuple-element.15.refs_2_), custom_call_target="tpu_custom_call" | custom-call | tf_op jit(solution)/shard_map/pallas_call | solution.py:656
